TPU v7x, 32 devices: a whole 2x2x4 slice. The times are simulated.
32 devices in a mesh: src: 4 (over y, x), space: 8 (over z, core).
Axes of the slice: x: 2, y: 2, z: 4, core: 2. Of those that a mesh axis runs over, the one named last changes fastest.
Arguments:
- vectors: bfloat16 [3, 2, 9216, 128], P(None, None, 'space', 'src'), may hold values from -0.0625 to 0.0625
- lambdas: float32 [3, 128], replicated, may hold values from 0.01 to 0.2
- sources: bfloat16 [2, 9216, 512], P(None, 'space', 'src'), may hold values from -6 to 6
Outputs:
- propagated: bfloat16 [2, 9216, 512], P(None, 'space', 'src')
All inputs are finite; a program needn't handle non-finite values.
Results may differ from a plain program's by a relative error of at most 0.0049.
Values may be sent and summed in bfloat16 or wider, within the bound.
No kernel may reach another device: no remote copies, remote signals or barrier semaphores. Data moves between devices by JAX's collectives and lax.ppermute only.
A program may use at most 64 MiB of HBM per device.

v0:
```python
import jax
import jax.numpy as jnp
from jax import lax
from jax.sharding import PartitionSpec as P


def project(vec_re, vec_im, src_re, src_im):
    coef_re = jnp.einsum(
        "rm,rc->mc", vec_re, src_re, preferred_element_type=jnp.float32
    ) + jnp.einsum("rm,rc->mc", vec_im, src_im, preferred_element_type=jnp.float32)
    coef_im = jnp.einsum(
        "rm,rc->mc", vec_re, src_im, preferred_element_type=jnp.float32
    ) - jnp.einsum("rm,rc->mc", vec_im, src_re, preferred_element_type=jnp.float32)
    return (coef_re, coef_im)


def scaled_coeffs(pair, lambda_rows):
    inverse = 1.0 / lambda_rows
    summed = lax.psum(pair, "space")
    scaled = (summed * inverse[None, :, :, None]).astype(jnp.bfloat16)
    return scaled


def expand(vec_re, vec_im, scaled_re, scaled_im, out_re, out_im):
    out_re = (
        out_re
        + jnp.dot(vec_re, scaled_re, preferred_element_type=jnp.float32)
        - jnp.dot(vec_im, scaled_im, preferred_element_type=jnp.float32)
    )
    out_im = (
        out_im
        + jnp.dot(vec_re, scaled_im, preferred_element_type=jnp.float32)
        + jnp.dot(vec_im, scaled_re, preferred_element_type=jnp.float32)
    )
    return (out_re, out_im)


def on_device(vectors, lambdas, sources):
    src_re = sources[0]
    src_im = sources[1]
    blocks = vectors.shape[0]
    out_re = jnp.zeros(src_re.shape, jnp.float32)
    out_im = jnp.zeros(src_re.shape, jnp.float32)
    for number in range(blocks):
        whole_block = lax.all_gather(vectors[number], "src", axis=2, tiled=True)
        partial_re, partial_im = project(whole_block[0], whole_block[1], src_re, src_im)
        pair = jnp.stack([partial_re, partial_im])[:, None]
        scaled = scaled_coeffs(pair, lambdas[number][None, :])
        out_re, out_im = expand(
            whole_block[0], whole_block[1], scaled[0, 0], scaled[1, 0], out_re, out_im
        )
    return jnp.stack([out_re, out_im]).astype(jnp.bfloat16)


def solution(mesh):
    placed = (P(None, None, "space", "src"), P(), P(None, "space", "src"))
    return jax.shard_map(
        on_device, mesh=mesh, in_specs=placed, out_specs=P(None, "space", "src"), check_vma=False
    )
```

profile of v0, /device:TPU:0, one launch (start us, length us, event | category | flops | bytes accessed | tf_op | source)
XLA Modules:
  0.0 114.1 jit_solution(4130897695937442077)
XLA Ops:
  6.5 1.1 fusion.42
  7.6 11.9 %all-gather.2 = bf16[1,2,1152,128]{2,3,1,0:T(8,128)(2,1)S(1)} all-gather(bf16[1,2,1152,32]{2,3,1,0:T(8,128)(2,1)S(1)} %get-tuple-element.8), channel_id=4, replica_groups=mesh['src'=4,'space'=8] {'src'}, dimensions={3}, use_global_device_ids=true | all-gather | bytes 737280 | tf_op jit(solution)/shard_map/all_gather | solution.py:45
  19.5 0.2 fusion.10
  20.0 10.7 %all-gather = bf16[1,2,1152,128]{2,3,1,0:T(8,128)(2,1)S(1)} all-gather(bf16[1,2,1152,32]{2,3,1,0:T(8,128)(2,1)S(1)} %get-tuple-element.9), channel_id=2, replica_groups=mesh['src'=4,'space'=8] {'src'}, dimensions={3}, use_global_device_ids=true | all-gather | bytes 737280 | tf_op jit(solution)/shard_map/all_gather | solution.py:45
  30.7 0.2 fusion.16
  31.2 9.7 %all-gather.1 = bf16[1,2,1152,128]{2,3,1,0:T(8,128)(2,1)S(1)} all-gather(bf16[1,2,1152,32]{2,3,1,0:T(8,128)(2,1)S(1)} %get-tuple-element.10), channel_id=3, replica_groups=mesh['src'=4,'space'=8] {'src'}, dimensions={3}, use_global_device_ids=true | all-gather | bytes 737280 | tf_op jit(solution)/shard_map/all_gather | solution.py:45
  40.9 0.2 fusion.13
  41.7 0.2 fusion.5
  41.9 0.2 fusion.8
  42.2 0.2 fusion.9
  42.4 0.2 fusion.6
  42.6 0.2 fusion.7
  42.9 0.7 maximum_bitcast_fusion.2
  43.5 0.7 maximum_bitcast_fusion
  44.2 0.7 maximum_bitcast_fusion.1
  44.9 0.7 copy-done.2
  45.6 55.6 %all-reduce.3.cloned.1.call-done = (f32[2,1,128,128]{3,2,0,1:T(8,128)}, f32[2,1,128,128]{3,2,0,1:T(8,128)}, f32[2,1,128,128]{3,2,0,1:T(8,128)}) async-done(((f32[2,1,128,128]{3,2,0,1:T(8,128)}, f32[2,1,128,128]{3,2,0,1:T(8,128)}, f32[2,1,128,128]{3,2,0,1:T(8,128)}), (f32[2,1,128,128]{3,2,0,1:T(8,128)}, f32[2,1,128,128]{3,2,0,1:T(8,128)}, f32[2,1,128,128]{3,2,0,1:T(8,128)})) %all-reduce.3.cloned.1.call-update) | async-done | bytes 393232 | tf_op jit(solution)/shard_map/psum | solution.py:19
  101.1 1.0 multiply_convert_fusion.2
  102.1 0.3 fusion.28
  102.4 0.3 fusion.29
  102.7 0.3 convolution_add_fusion.4
  102.9 0.6 copy-done
  103.7 0.3 convolution_add_fusion.3
  104.0 0.3 convolution_add_fusion.2
  104.3 0.3 convolution_add_fusion.1
  104.5 0.3 fusion.2
  104.8 0.3 convolution_subtract_fusion.2
  105.1 0.3 convolution_add_fusion.6
  105.3 0.3 convolution_subtract_fusion.1
  105.6 0.3 convolution_add_fusion.5
  105.9 0.3 fusion.3
  106.2 1.1 copy.4
  (15 shorter events, 1.2 us)
Async XLA Ops:
  6.5 94.6 %all-reduce.3.cloned.1.call-start = ((), (), s32[]{:S(2)}) async-start(), calls=%async_computation | async-start | bytes 786432 | tf_op jit(solution)/shard_map/psum | solution.py:19
  7.6 11.9 %copy-start.3 = (bf16[2,1152,128]{2,1,0:T(8,128)(2,1)S(1)}, bf16[2,1152,128]{2,1,0:T(8,128)(2,1)}, u32[]{:S(2)}) copy-start(bf16[2,1152,128]{2,1,0:T(8,128)(2,1)} %param.5) | copy-start | bytes 1769476
  44.9 0.7 copy-start.2
  102.7 0.9 copy-start
  102.7 1.0 copy-start.1
Sparse Core Ops, SparseCore 0:
  45.0 56.0 all-reduce.2
where the time goes:
time: 114 us
  waiting for transfers between devices  55.6 us (49%)
  blocking collectives  32.3 us (28%)
  between operations  13.6 us (12%)
  matrix products  5.97 us (5%)
  local copies, waits for them, and re-layouts  3.5 us (3%)
  other arithmetic  3.13 us (3%)
    psum x1, waiting for transfers between devices, scaled_coeffs(): summed = lax.psum(pair, 'space')  55.6 us
    all_gather x3, blocking collectives, on_device(): whole_block = lax.all_gather(vectors[number], 'src', axis=2, tiled=True)  32.3 us
  transfers between devices with their start and end apart: 1, of which 1 were waited for; matrix products, arithmetic and copies ran while one was open for 0% of the time, Pallas kernels for 0%

commit v1 on v0

v1 whole, which is shorter than its diff:
```python
import functools

import jax
import jax.numpy as jnp
from jax import lax
from jax.experimental import pallas as pl
from jax.experimental.pallas import tpu as pltpu
from jax.sharding import PartitionSpec as P

VMEM = pl.BlockSpec(memory_space=pltpu.VMEM)
LIMIT = 40 * 1024 * 1024


def call(body, outs, args, flops=0):
    moved = sum(a.size * a.dtype.itemsize for a in list(args) + list(outs))
    return pl.pallas_call(
        body,
        out_shape=outs,
        in_specs=[VMEM] * len(args),
        out_specs=[VMEM] * len(outs),
        compiler_params=pltpu.CompilerParams(vmem_limit_bytes=LIMIT),
        cost_estimate=pl.CostEstimate(flops=flops, bytes_accessed=moved, transcendentals=0),
    )(*args)


def inverse_body(lam_ref, inv_ref):
    blocks, modes, cols = inv_ref.shape
    inverse = 1.0 / lam_ref[...]
    for k in range(blocks):
        inv_ref[k] = jnp.broadcast_to(inverse[k : k + 1, :], (cols, modes)).T


def project_body(count, *refs):
    pieces, (src_ref, mine_ref, theirs_ref) = refs[:count], refs[count:]
    keeps_real = lax.axis_index("space") % 2 == 0
    both = jnp.concatenate([src_ref[0], src_ref[1]], axis=1)
    cols = src_ref.shape[2]
    for i, piece in enumerate(pieces):
        blocks, _, modes, rows = piece.shape
        flat = piece[...].reshape(blocks * 2 * modes, rows)
        prod = jnp.dot(flat, both, preferred_element_type=jnp.float32)
        prod = prod.reshape(blocks, 2, modes, 2 * cols)
        real = prod[:, 0, :, :cols] + prod[:, 1, :, cols:]
        imag = prod[:, 0, :, cols:] - prod[:, 1, :, :cols]
        mine_ref[i] = jnp.where(keeps_real, real, imag)
        theirs_ref[i] = jnp.where(keeps_real, imag, real)


def add_body(*refs):
    total = refs[0][...]
    for ref in refs[1:-1]:
        total = total + ref[...]
    refs[-1][...] = total


def scale_body(places, per_device, *refs):
    parts, (inv_ref, out_ref) = refs[:-2], refs[-2:]
    me = lax.axis_index("src")
    _, blocks, modes, _ = out_ref.shape
    for i, (source, first) in enumerate(places):
        start = pl.multiple_of(source(me) * per_device + first, 8)
        total = parts[0][i]
        for part in parts[1:]:
            total = total + part[i]
        for k in range(blocks):
            factor = inv_ref[k, pl.ds(start, modes), :]
            out_ref[i, k] = (total[k] * factor).astype(out_ref.dtype)


def expand_body(counts, *refs):
    out_ref = refs[-1]
    keeps_real = lax.axis_index("space") % 2 == 0
    left, right, at = [], [], 0
    for count in counts:
        pieces, (mine_ref, theirs_ref) = refs[at : at + count], refs[at + count : at + count + 2]
        at += count + 2
        for i, piece in enumerate(pieces):
            blocks, _, modes, rows = piece.shape
            left.append(piece[...].reshape(blocks * 2 * modes, rows))
            mine, theirs = mine_ref[i], theirs_ref[i]
            real = jnp.where(keeps_real, mine, theirs)
            imag = jnp.where(keeps_real, theirs, mine)
            for k in range(blocks):
                right.append(jnp.concatenate([real[k], imag[k]], axis=1))
                right.append(jnp.concatenate([-imag[k], real[k]], axis=1))
    left = jnp.concatenate(left, axis=0)
    right = jnp.concatenate(right, axis=0)
    cols = out_ref.shape[2]
    out = lax.dot_general(left, right, (((0,), (0,)), ((), ())), preferred_element_type=jnp.float32)
    out_ref[0] = out[:, :cols].astype(out_ref.dtype)
    out_ref[1] = out[:, cols:].astype(out_ref.dtype)


def swap(x, axis, size, bit):
    return lax.ppermute(x, axis, [(i, i ^ bit) for i in range(size)])


def gather_pieces(own, n_src):
    modes = own.shape[2]
    if n_src == 4:
        half = modes // 2
        low, high = own[:, :, :half], own[:, :, half:]
        x = functools.partial(swap, axis="src", size=4, bit=1)
        y = functools.partial(swap, axis="src", size=4, bit=2)
        x_low, y_high = x(low), y(high)
        x_high, y_low = x(high), y(low)
        d_low, d_high = y(x_low), x(y_high)
        at = lambda q: lambda me: me ^ q
        return [
            [(low, at(0), 0), (high, at(0), half), (x_low, at(1), 0), (y_high, at(2), half)],
            [(x_high, at(1), half), (y_low, at(2), 0), (d_low, at(3), 0), (d_high, at(3), half)],
        ]
    group = [(own, lambda me: me, 0)]
    for step in range(1, n_src):
        piece = lax.ppermute(own, "src", [(i, (i + step) % n_src) for i in range(n_src)])
        group.append((piece, lambda me, step=step: (me + n_src - step) % n_src, 0))
    return [group]


def reduce_group(group, sources, inv, per_device, n_space):
    pieces = [p for p, _, _ in group]
    places = [(source, first) for _, source, first in group]
    blocks, _, modes, rows = pieces[0].shape
    cols = sources.shape[2]
    shape = (len(pieces), blocks, modes, cols)
    part = jax.ShapeDtypeStruct(shape, jnp.float32)
    mine, theirs = call(
        functools.partial(project_body, len(pieces)),
        [part, part],
        pieces + [sources],
        flops=8 * len(pieces) * blocks * modes * rows * cols,
    )
    arrived = swap(theirs, "space", n_space, 1)
    (total,) = call(add_body, [part], [mine, arrived])
    if n_space == 8:
        parts = [total] + [swap(total, "space", n_space, bit) for bit in (2, 4, 6)]
    else:
        bit = 2
        while bit < n_space:
            parts = [total, swap(total, "space", n_space, bit)]
            bit *= 2
            if bit < n_space:
                (total,) = call(add_body, [part], parts)
    (scaled,) = call(
        functools.partial(scale_body, places, per_device),
        [jax.ShapeDtypeStruct(shape, jnp.bfloat16)],
        parts + [inv],
    )
    return pieces, scaled, swap(scaled, "space", n_space, 1)


def on_device(n_src, n_space, vectors, lambdas, sources):
    own = jnp.swapaxes(vectors, 2, 3)
    blocks, _, per_device, rows = own.shape
    cols = sources.shape[2]
    (inv,) = call(inverse_body, [jax.ShapeDtypeStruct(lambdas.shape + (cols,), jnp.float32)], [lambdas])
    counts, args = [], []
    for group in gather_pieces(own, n_src):
        pieces, mine, theirs = reduce_group(group, sources, inv, per_device, n_space)
        counts.append(len(pieces))
        args += pieces + [mine, theirs]
    (out,) = call(
        functools.partial(expand_body, counts),
        [jax.ShapeDtypeStruct(sources.shape, jnp.bfloat16)],
        args,
        flops=8 * blocks * per_device * n_src * rows * cols,
    )
    return out


def solution(mesh):
    sizes = dict(mesh.shape)
    placed = (P(None, None, "space", "src"), P(), P(None, "space", "src"))
    return jax.shard_map(
        functools.partial(on_device, sizes["src"], sizes["space"]),
        mesh=mesh,
        in_specs=placed,
        out_specs=P(None, "space", "src"),
        check_vma=False,
    )
```

time: 114 us -> 45.2 us (0.40)
  waiting for transfers between devices: 55.6 us -> 20.7 us
  blocking collectives: 32.3 us -> 0 us
  starting transfers between devices: 0.01 us -> 20.3 us
  between operations: 13.6 us -> 0.12 us
  matrix products: 5.97 us -> 0 us
  other arithmetic: 3.13 us -> 0 us
  Pallas kernels: 0 us -> 2.77 us
  local copies, waits for them, and re-layouts: 3.5 us -> 1.15 us
    psum x1 -> x0, waiting for transfers between devices: 55.6 us -> none  [scaled_coeffs(): summed = lax.psum(pair, 'space')]
    all_gather x3 -> x0, blocking collectives: 32.3 us -> none  [on_device(): whole_block = lax.all_gather(vectors[number], 'src', axis=2, tiled=True)]
    ppermute x0 -> x16, waiting for transfers between devices: none -> 20.7 us  [swap(): return lax.ppermute(x, axis, [(i, i ^ bit) for i in range(size)])]
    ppermute x0 -> x16, starting transfers between devices: none -> 20.3 us  [swap(): return lax.ppermute(x, axis, [(i, i ^ bit) for i in range(size)])]
    dot_general x24 -> x0, matrix products: 5.97 us -> none  [the longest x3 0.78 us: expand(): jnp.dot(vec_im, scaled_re, preferred_element_type=jnp.float32)]
    pallas_call x0 -> x8, Pallas kernels: none -> 2.77 us  [call(): pl.pallas_call(body, out_shape=outs, in_specs=[VMEM] * len(args), out_spe...]
    broadcast_in_dim x3 -> x0, other arithmetic: 1.98 us -> none  [on_device(): pair = jnp.stack([partial_re, partial_im])[:, None]]
    unnamed x8 -> x4, local copies, waits for them, and re-layouts: 1.35 us -> 0.01 us
  transfers between devices with their start and end apart: 1 -> 16, of which waited for: 1 -> 7; matrix products, arithmetic and copies ran while one was open for 0% -> 0% of each run, Pallas kernels for 0% -> 3%
where the time goes in v1:
time: 45.2 us; the launch traced here: 45.1 us
  waiting for transfers between devices  20.7 us (46%)
  starting transfers between devices  20.3 us (45%)
  Pallas kernels  2.77 us (6%)
  local copies, waits for them, and re-layouts  1.15 us (3%)
    ppermute x16, waiting for transfers between devices, swap(): return lax.ppermute(x, axis, [(i, i ^ bit) for i in range(size)])  20.7 us
    ppermute x16, starting transfers between devices, swap(): return lax.ppermute(x, axis, [(i, i ^ bit) for i in range(size)])  20.3 us
    pallas_call x8, Pallas kernels, call(): pl.pallas_call(body, out_shape=outs, in_specs=[VMEM] * len(args), out_spe...  2.77 us
    slice x1, local copies, waits for them, and re-layouts, gather_pieces(): low, high = (own[:, :, :half], own[:, :, half:])  1.14 us
  transfers between devices with their start and end apart: 16, of which 7 were waited for; matrix products, arithmetic and copies ran while one was open for 0% of the time, Pallas kernels for 3%

profile of v1, /device:TPU:0, one launch (start us, length us, event | category | flops | bytes accessed | tf_op | source)
XLA Modules:
  0.0 45.1 jit_solution(3598446521585213207)
XLA Ops:
  0.0 1.1 %fusion = (bf16[3,2,16,1152]{3,2,1,0:T(8,128)(2,1)S(1)}, bf16[3,2,16,1152]{3,2,1,0:T(8,128)(2,1)S(1)}) fusion(bf16[3,2,32,1152]{3,2,1,0:T(8,128)(2,1)} %bitcast.1), kind=kLoop, calls=%fused_computation | loop fusion | bytes 884736 | tf_op jit(solution)/shard_map/slice | solution.py:102
  1.1 3.0 %collective-permute-start.1 = (bf16[3,2,16,1152]{3,2,1,0:T(8,128)(2,1)S(1)}, bf16[3,2,16,1152]{3,2,1,0:T(8,128)(2,1)S(1)}, u32[]{:S(2)}, u32[]{:S(2)}) collective-permute-start(bf16[3,2,16,1152]{3,2,1,0:T(8,128)(2,1)S(1)} %get-tuple-element.13.refs_1_), channel_id=1, source_target_pairs={{0,16},{8,24},{16,0},{24,8},{1,17},{9,25},{17,1},{25,9},{2,18},{10... | collective-permute-start | bytes 663560 | tf_op jit(solution)/shard_map/ppermute | solution.py:95
  4.2 1.5 %collective-permute-start = (bf16[3,2,16,1152]{3,2,1,0:T(8,128)(2,1)S(1)}, bf16[3,2,16,1152]{3,2,1,0:T(8,128)(2,1)S(1)}, u32[]{:S(2)}, u32[]{:S(2)}) collective-permute-start(bf16[3,2,16,1152]{3,2,1,0:T(8,128)(2,1)S(1)} %get-tuple-element.14.refs_0_), channel_id=1, source_target_pairs={{0,8},{8,0},{16,24},{24,16},{1,9},{9,1},{17,25},{25,17},{2,10},{10... | collective-permute-start | bytes 663560 | tf_op jit(solution)/shard_map/ppermute | solution.py:95
  5.7 0.5 %collective-permute-start.7 = (bf16[3,2,16,1152]{3,2,1,0:T(8,128)(2,1)S(1)}, bf16[3,2,16,1152]{3,2,1,0:T(8,128)(2,1)S(1)}, u32[]{:S(2)}, u32[]{:S(2)}) collective-permute-start(bf16[3,2,16,1152]{3,2,1,0:T(8,128)(2,1)S(1)} %get-tuple-element.13.refs_1_), channel_id=1, source_target_pairs={{0,8},{8,0},{16,24},{24,16},{1,9},{9,1},{17,25},{25,17},{2,10},{10... | collective-permute-start | bytes 663560 | tf_op jit(solution)/shard_map/ppermute | solution.py:95
  6.2 0.1 collective-permute-start.8
  6.3 4.2 %collective-permute-done.1.refs_3_ = bf16[3,2,16,1152]{3,2,1,0:T(8,128)(2,1)S(1)} collective-permute-done((bf16[3,2,16,1152]{3,2,1,0:T(8,128)(2,1)S(1)}, bf16[3,2,16,1152]{3,2,1,0:T(8,128)(2,1)S(1)}, u32[]{:S(2)}, u32[]{:S(2)}) %collective-permute-start.1) | collective-permute-done | bytes 221216 | tf_op jit(solution)/shard_map/ppermute | solution.py:95
  10.4 2.0 %collective-permute-start.10 = (bf16[3,2,16,1152]{3,2,1,0:T(8,128)(2,1)S(1)}, bf16[3,2,16,1152]{3,2,1,0:T(8,128)(2,1)S(1)}, u32[]{:S(2)}, u32[]{:S(2)}) collective-permute-start(bf16[3,2,16,1152]{3,2,1,0:T(8,128)(2,1)S(1)} %collective-permute-done.1.refs_3_), channel_id=1, source_target_pairs={{0,8},{8,0},{16,24},{24,16},{1,9},{9,1},{17,25},{25,17},{2,10},{10... | collective-permute-start | bytes 663560 | tf_op jit(solution)/shard_map/ppermute | solution.py:95
  12.5 0.1 collective-permute-done.refs_2_
  12.5 1.5 %collective-permute-start.9 = (bf16[3,2,16,1152]{3,2,1,0:T(8,128)(2,1)S(1)}, bf16[3,2,16,1152]{3,2,1,0:T(8,128)(2,1)S(1)}, u32[]{:S(2)}, u32[]{:S(2)}) collective-permute-start(bf16[3,2,16,1152]{3,2,1,0:T(8,128)(2,1)S(1)} %collective-permute-done.refs_2_), channel_id=1, source_target_pairs={{0,16},{8,24},{16,0},{24,8},{1,17},{9,25},{17,1},{25,9},{2,18},{10... | collective-permute-start | bytes 663560 | tf_op jit(solution)/shard_map/ppermute | solution.py:95
  14.0 0.5 %shard_map.37 = (f32[4,3,16,128]{3,2,1,0:T(8,128)S(1)}, f32[4,3,16,128]{3,2,1,0:T(8,128)S(1)}) custom-call(bf16[3,2,16,1152]{3,2,1,0:T(8,128)(2,1)S(1)} %get-tuple-element.14.refs_0_, bf16[3,2,16,1152]{3,2,1,0:T(8,128)(2,1)S(1)} %get-tuple-element.13.refs_1_, bf16[3,2,16,1152]{3,2,1,0:T(8,128)(2,1)S(1)} %collective-permute-done.refs_2_, ...), custom_call_target="tpu_custom_call" | custom-call | flops 226492416 | bytes 1671168 | tf_op jit(solution)/shard_map/pallas_call | solution.py:16
  14.5 0.1 collective-permute-start.2
  14.6 2.7 %collective-permute-done.7.refs_0_.refs_6_ = bf16[3,2,16,1152]{3,2,1,0:T(8,128)(2,1)S(1)} collective-permute-done((bf16[3,2,16,1152]{3,2,1,0:T(8,128)(2,1)S(1)}, bf16[3,2,16,1152]{3,2,1,0:T(8,128)(2,1)S(1)}, u32[]{:S(2)}, u32[]{:S(2)}) %collective-permute-start.7) | collective-permute-done | bytes 221216 | tf_op jit(solution)/shard_map/ppermute | solution.py:95
  17.3 0.0 collective-permute-done.8.refs_1_.refs_7_
  17.3 3.3 %collective-permute-done.10.refs_3_.refs_9_ = bf16[3,2,16,1152]{3,2,1,0:T(8,128)(2,1)S(1)} collective-permute-done((bf16[3,2,16,1152]{3,2,1,0:T(8,128)(2,1)S(1)}, bf16[3,2,16,1152]{3,2,1,0:T(8,128)(2,1)S(1)}, u32[]{:S(2)}, u32[]{:S(2)}) %collective-permute-start.10) | collective-permute-done | bytes 221216 | tf_op jit(solution)/shard_map/ppermute | solution.py:95
  20.6 0.5 %shard_map.41 = (f32[4,3,16,128]{3,2,1,0:T(8,128)S(1)}, f32[4,3,16,128]{3,2,1,0:T(8,128)S(1)}) custom-call(bf16[3,2,16,1152]{3,2,1,0:T(8,128)(2,1)S(1)} %collective-permute-done.7.refs_0_.refs_6_, bf16[3,2,16,1152]{3,2,1,0:T(8,128)(2,1)S(1)} %collective-permute-done.8.refs_1_.refs_7_, bf16[3,2,16,1152]{3,2,1,0:T(8,128)(2,1)S(1)} %collective-permute-done.9.refs_2_.refs_8_, ...), custom_call_target="tpu_custom_call" | custom-call | flops 226492416 | bytes 1671168 | tf_op jit(solution)/shard_map/pallas_call | solution.py:16
  21.1 0.1 collective-permute-start.11
  21.2 0.0 collective-permute-done.2.refs_1_
  21.2 3.7 %collective-permute-start.5 = (f32[4,3,16,128]{3,2,1,0:T(8,128)S(1)}, f32[4,3,16,128]{3,2,1,0:T(8,128)S(1)}, u32[]{:S(2)}, u32[]{:S(2)}) collective-permute-start(f32[4,3,16,128]{3,2,1,0:T(8,128)S(1)} %shard_map.38.refs_0_), channel_id=1, source_target_pairs={{0,6},{1,7},{2,4},{3,5},{4,2},{5,3},{6,0},{7,1},{8,14},{9,15},{10,... | collective-permute-start | bytes 294920 | tf_op jit(solution)/shard_map/ppermute | solution.py:95
  24.9 0.8 %collective-permute-start.3 = (f32[4,3,16,128]{3,2,1,0:T(8,128)S(1)}, f32[4,3,16,128]{3,2,1,0:T(8,128)S(1)}, u32[]{:S(2)}, u32[]{:S(2)}) collective-permute-start(f32[4,3,16,128]{3,2,1,0:T(8,128)S(1)} %shard_map.38.refs_0_), channel_id=1, source_target_pairs={{0,2},{1,3},{2,0},{3,1},{4,6},{5,7},{6,4},{7,5},{8,10},{9,11},{10,... | collective-permute-start | bytes 294920 | tf_op jit(solution)/shard_map/ppermute | solution.py:95
  25.7 3.7 %collective-permute-start.14 = (f32[4,3,16,128]{3,2,1,0:T(8,128)S(1)}, f32[4,3,16,128]{3,2,1,0:T(8,128)S(1)}, u32[]{:S(2)}, u32[]{:S(2)}) collective-permute-start(f32[4,3,16,128]{3,2,1,0:T(8,128)S(1)} %shard_map.42.refs_0_), channel_id=1, source_target_pairs={{0,6},{1,7},{2,4},{3,5},{4,2},{5,3},{6,0},{7,1},{8,14},{9,15},{10,... | collective-permute-start | bytes 294920 | tf_op jit(solution)/shard_map/ppermute | solution.py:95
  29.4 0.0 collective-permute-start.13
  29.4 0.0 collective-permute-done.5.refs_3_
  29.4 3.3 %collective-permute-start.12 = (f32[4,3,16,128]{3,2,1,0:T(8,128)S(1)}, f32[4,3,16,128]{3,2,1,0:T(8,128)S(1)}, u32[]{:S(2)}, u32[]{:S(2)}) collective-permute-start(f32[4,3,16,128]{3,2,1,0:T(8,128)S(1)} %shard_map.42.refs_0_), channel_id=1, source_target_pairs={{0,2},{1,3},{2,0},{3,1},{4,6},{5,7},{6,4},{7,5},{8,10},{9,11},{10,... | collective-permute-start | bytes 294920 | tf_op jit(solution)/shard_map/ppermute | solution.py:95
  32.7 0.1 shard_map.39.refs_4_
  32.8 5.6 %collective-permute-done.4.refs_2_ = f32[4,3,16,128]{3,2,1,0:T(8,128)S(1)} collective-permute-done((f32[4,3,16,128]{3,2,1,0:T(8,128)S(1)}, f32[4,3,16,128]{3,2,1,0:T(8,128)S(1)}, u32[]{:S(2)}, u32[]{:S(2)}) %collective-permute-start.4) | collective-permute-done | bytes 98336 | tf_op jit(solution)/shard_map/ppermute | solution.py:95
  38.4 0.0 collective-permute-done.3.refs_1_
  38.5 0.1 collective-permute-start.6
  38.6 3.7 %collective-permute-done.13.refs_2_ = f32[4,3,16,128]{3,2,1,0:T(8,128)S(1)} collective-permute-done((f32[4,3,16,128]{3,2,1,0:T(8,128)S(1)}, f32[4,3,16,128]{3,2,1,0:T(8,128)S(1)}, u32[]{:S(2)}, u32[]{:S(2)}) %collective-permute-start.13) | collective-permute-done | bytes 98336 | tf_op jit(solution)/shard_map/ppermute | solution.py:95
  42.3 0.1 collective-permute-start.15
  42.3 0.0 collective-permute-done.6.refs_5_
  42.4 1.2 %collective-permute-done.15.refs_11_ = bf16[4,3,16,128]{3,2,1,0:T(8,128)(2,1)S(1)} collective-permute-done((bf16[4,3,16,128]{3,2,1,0:T(8,128)(2,1)S(1)}, bf16[4,3,16,128]{3,2,1,0:T(8,128)(2,1)S(1)}, u32[]{:S(2)}, u32[]{:S(2)}) %collective-permute-start.15) | collective-permute-done | bytes 49184 | tf_op jit(solution)/shard_map/ppermute | solution.py:95
  43.6 1.5 %shard_map.44 = bf16[2,1152,128]{2,1,0:T(8,128)(2,1)} custom-call(bf16[3,2,16,1152]{3,2,1,0:T(8,128)(2,1)S(1)} %get-tuple-element.14.refs_0_, bf16[3,2,16,1152]{3,2,1,0:T(8,128)(2,1)S(1)} %get-tuple-element.13.refs_1_, bf16[3,2,16,1152]{3,2,1,0:T(8,128)(2,1)S(1)} %collective-permute-done.refs_2_, ...), custom_call_target="tpu_custom_call" | custom-call | flops 452984832 | bytes 2555904 | tf_op jit(solution)/shard_map/pallas_call | solution.py:16
  (13 shorter events, 0.1 us)
Async XLA Ops:
  0.0 14.0 %copy-start = (bf16[2,1152,128]{2,1,0:T(8,128)(2,1)S(1)}, bf16[2,1152,128]{2,1,0:T(8,128)(2,1)}, u32[]{:S(2)}) copy-start(bf16[2,1152,128]{2,1,0:T(8,128)(2,1)} %refs_4_.3) | copy-start | bytes 1769476
  1.1 9.3 %collective-permute-start.1 = (bf16[3,2,16,1152]{3,2,1,0:T(8,128)(2,1)S(1)}, bf16[3,2,16,1152]{3,2,1,0:T(8,128)(2,1)S(1)}, u32[]{:S(2)}, u32[]{:S(2)}) collective-permute-start(bf16[3,2,16,1152]{3,2,1,0:T(8,128)(2,1)S(1)} %get-tuple-element.13.refs_1_), channel_id=1, source_target_pairs={{0,16},{8,24},{16,0},{24,8},{1,17},{9,25},{17,1},{25,9},{2,18},{10... | collective-permute-start | bytes 663560 | tf_op jit(solution)/shard_map/ppermute | solution.py:95
  4.2 8.4 %collective-permute-start = (bf16[3,2,16,1152]{3,2,1,0:T(8,128)(2,1)S(1)}, bf16[3,2,16,1152]{3,2,1,0:T(8,128)(2,1)S(1)}, u32[]{:S(2)}, u32[]{:S(2)}) collective-permute-start(bf16[3,2,16,1152]{3,2,1,0:T(8,128)(2,1)S(1)} %get-tuple-element.14.refs_0_), channel_id=1, source_target_pairs={{0,8},{8,0},{16,24},{24,16},{1,9},{9,1},{17,25},{25,17},{2,10},{10... | collective-permute-start | bytes 663560 | tf_op jit(solution)/shard_map/ppermute | solution.py:95
  5.7 11.6 %collective-permute-start.7 = (bf16[3,2,16,1152]{3,2,1,0:T(8,128)(2,1)S(1)}, bf16[3,2,16,1152]{3,2,1,0:T(8,128)(2,1)S(1)}, u32[]{:S(2)}, u32[]{:S(2)}) collective-permute-start(bf16[3,2,16,1152]{3,2,1,0:T(8,128)(2,1)S(1)} %get-tuple-element.13.refs_1_), channel_id=1, source_target_pairs={{0,8},{8,0},{16,24},{24,16},{1,9},{9,1},{17,25},{25,17},{2,10},{10... | collective-permute-start | bytes 663560 | tf_op jit(solution)/shard_map/ppermute | solution.py:95
  6.2 11.1 %collective-permute-start.8 = (bf16[3,2,16,1152]{3,2,1,0:T(8,128)(2,1)S(1)}, bf16[3,2,16,1152]{3,2,1,0:T(8,128)(2,1)S(1)}, u32[]{:S(2)}, u32[]{:S(2)}) collective-permute-start(bf16[3,2,16,1152]{3,2,1,0:T(8,128)(2,1)S(1)} %get-tuple-element.14.refs_0_), channel_id=1, source_target_pairs={{0,16},{8,24},{16,0},{24,8},{1,17},{9,25},{17,1},{25,9},{2,18},{10... | collective-permute-start | bytes 663560 | tf_op jit(solution)/shard_map/ppermute | solution.py:95
  10.4 10.1 %collective-permute-start.10 = (bf16[3,2,16,1152]{3,2,1,0:T(8,128)(2,1)S(1)}, bf16[3,2,16,1152]{3,2,1,0:T(8,128)(2,1)S(1)}, u32[]{:S(2)}, u32[]{:S(2)}) collective-permute-start(bf16[3,2,16,1152]{3,2,1,0:T(8,128)(2,1)S(1)} %collective-permute-done.1.refs_3_), channel_id=1, source_target_pairs={{0,8},{8,0},{16,24},{24,16},{1,9},{9,1},{17,25},{25,17},{2,10},{10... | collective-permute-start | bytes 663560 | tf_op jit(solution)/shard_map/ppermute | solution.py:95
  12.5 8.0 %collective-permute-start.9 = (bf16[3,2,16,1152]{3,2,1,0:T(8,128)(2,1)S(1)}, bf16[3,2,16,1152]{3,2,1,0:T(8,128)(2,1)S(1)}, u32[]{:S(2)}, u32[]{:S(2)}) collective-permute-start(bf16[3,2,16,1152]{3,2,1,0:T(8,128)(2,1)S(1)} %collective-permute-done.refs_2_), channel_id=1, source_target_pairs={{0,16},{8,24},{16,0},{24,8},{1,17},{9,25},{17,1},{25,9},{2,18},{10... | collective-permute-start | bytes 663560 | tf_op jit(solution)/shard_map/ppermute | solution.py:95
  14.5 6.6 %collective-permute-start.2 = (f32[4,3,16,128]{3,2,1,0:T(8,128)S(1)}, f32[4,3,16,128]{3,2,1,0:T(8,128)S(1)}, u32[]{:S(2)}, u32[]{:S(2)}) collective-permute-start(f32[4,3,16,128]{3,2,1,0:T(8,128)S(1)} %get-tuple-element.10), channel_id=1, source_target_pairs={{0,1},{1,0},{2,3},{3,2},{4,5},{5,4},{6,7},{7,6},{8,9},{9,8},{10,11... | collective-permute-start | bytes 294920 | tf_op jit(solution)/shard_map/ppermute | solution.py:95
  21.1 4.6 %collective-permute-start.11 = (f32[4,3,16,128]{3,2,1,0:T(8,128)S(1)}, f32[4,3,16,128]{3,2,1,0:T(8,128)S(1)}, u32[]{:S(2)}, u32[]{:S(2)}) collective-permute-start(f32[4,3,16,128]{3,2,1,0:T(8,128)S(1)} %get-tuple-element.12), channel_id=1, source_target_pairs={{0,1},{1,0},{2,3},{3,2},{4,5},{5,4},{6,7},{7,6},{8,9},{9,8},{10,11... | collective-permute-start | bytes 294920 | tf_op jit(solution)/shard_map/ppermute | solution.py:95
  21.2 8.2 %collective-permute-start.5 = (f32[4,3,16,128]{3,2,1,0:T(8,128)S(1)}, f32[4,3,16,128]{3,2,1,0:T(8,128)S(1)}, u32[]{:S(2)}, u32[]{:S(2)}) collective-permute-start(f32[4,3,16,128]{3,2,1,0:T(8,128)S(1)} %shard_map.38.refs_0_), channel_id=1, source_target_pairs={{0,6},{1,7},{2,4},{3,5},{4,2},{5,3},{6,0},{7,1},{8,14},{9,15},{10,... | collective-permute-start | bytes 294920 | tf_op jit(solution)/shard_map/ppermute | solution.py:95
  24.9 13.6 %collective-permute-start.4 = (f32[4,3,16,128]{3,2,1,0:T(8,128)S(1)}, f32[4,3,16,128]{3,2,1,0:T(8,128)S(1)}, u32[]{:S(2)}, u32[]{:S(2)}) collective-permute-start(f32[4,3,16,128]{3,2,1,0:T(8,128)S(1)} %shard_map.38.refs_0_), channel_id=1, source_target_pairs={{0,4},{1,5},{2,6},{3,7},{4,0},{5,1},{6,2},{7,3},{8,12},{9,13},{10,... | collective-permute-start | bytes 294920 | tf_op jit(solution)/shard_map/ppermute | solution.py:95
  24.9 13.6 %collective-permute-start.3 = (f32[4,3,16,128]{3,2,1,0:T(8,128)S(1)}, f32[4,3,16,128]{3,2,1,0:T(8,128)S(1)}, u32[]{:S(2)}, u32[]{:S(2)}) collective-permute-start(f32[4,3,16,128]{3,2,1,0:T(8,128)S(1)} %shard_map.38.refs_0_), channel_id=1, source_target_pairs={{0,2},{1,3},{2,0},{3,1},{4,6},{5,7},{6,4},{7,5},{8,10},{9,11},{10,... | collective-permute-start | bytes 294920 | tf_op jit(solution)/shard_map/ppermute | solution.py:95
  25.7 7.0 %copy-start.1 = (f32[3,128]{1,0:T(4,128)S(1)}, f32[3,128]{1,0:T(4,128)}, u32[]{:S(2)}) copy-start(f32[3,128]{1,0:T(4,128)} %lam_ref.1) | copy-start | bytes 4612
  25.7 12.9 %collective-permute-start.14 = (f32[4,3,16,128]{3,2,1,0:T(8,128)S(1)}, f32[4,3,16,128]{3,2,1,0:T(8,128)S(1)}, u32[]{:S(2)}, u32[]{:S(2)}) collective-permute-start(f32[4,3,16,128]{3,2,1,0:T(8,128)S(1)} %shard_map.42.refs_0_), channel_id=1, source_target_pairs={{0,6},{1,7},{2,4},{3,5},{4,2},{5,3},{6,0},{7,1},{8,14},{9,15},{10,... | collective-permute-start | bytes 294920 | tf_op jit(solution)/shard_map/ppermute | solution.py:95
  29.4 12.9 %collective-permute-start.13 = (f32[4,3,16,128]{3,2,1,0:T(8,128)S(1)}, f32[4,3,16,128]{3,2,1,0:T(8,128)S(1)}, u32[]{:S(2)}, u32[]{:S(2)}) collective-permute-start(f32[4,3,16,128]{3,2,1,0:T(8,128)S(1)} %shard_map.42.refs_0_), channel_id=1, source_target_pairs={{0,4},{1,5},{2,6},{3,7},{4,0},{5,1},{6,2},{7,3},{8,12},{9,13},{10,... | collective-permute-start | bytes 294920 | tf_op jit(solution)/shard_map/ppermute | solution.py:95
  29.4 12.9 %collective-permute-start.12 = (f32[4,3,16,128]{3,2,1,0:T(8,128)S(1)}, f32[4,3,16,128]{3,2,1,0:T(8,128)S(1)}, u32[]{:S(2)}, u32[]{:S(2)}) collective-permute-start(f32[4,3,16,128]{3,2,1,0:T(8,128)S(1)} %shard_map.42.refs_0_), channel_id=1, source_target_pairs={{0,2},{1,3},{2,0},{3,1},{4,6},{5,7},{6,4},{7,5},{8,10},{9,11},{10,... | collective-permute-start | bytes 294920 | tf_op jit(solution)/shard_map/ppermute | solution.py:95
  38.5 3.9 %collective-permute-start.6 = (bf16[4,3,16,128]{3,2,1,0:T(8,128)(2,1)S(1)}, bf16[4,3,16,128]{3,2,1,0:T(8,128)(2,1)S(1)}, u32[]{:S(2)}, u32[]{:S(2)}) collective-permute-start(bf16[4,3,16,128]{3,2,1,0:T(8,128)(2,1)S(1)} %shard_map.40.refs_4_), channel_id=1, source_target_pairs={{0,1},{1,0},{2,3},{3,2},{4,5},{5,4},{6,7},{7,6},{8,9},{9,8},{10,11... | collective-permute-start | bytes 147464 | tf_op jit(solution)/shard_map/ppermute | solution.py:95
  42.3 1.3 %collective-permute-start.15 = (bf16[4,3,16,128]{3,2,1,0:T(8,128)(2,1)S(1)}, bf16[4,3,16,128]{3,2,1,0:T(8,128)(2,1)S(1)}, u32[]{:S(2)}, u32[]{:S(2)}) collective-permute-start(bf16[4,3,16,128]{3,2,1,0:T(8,128)(2,1)S(1)} %shard_map.43.refs_10_), channel_id=1, source_target_pairs={{0,1},{1,0},{2,3},{3,2},{4,5},{5,4},{6,7},{7,6},{8,9},{9,8},{10,11... | collective-permute-start | bytes 147464 | tf_op jit(solution)/shard_map/ppermute | solution.py:95

commit v2 on v0

v2 whole, which is shorter than its diff:
```python
import functools

import jax
import jax.numpy as jnp
from jax import lax
from jax.experimental import pallas as pl
from jax.experimental.pallas import tpu as pltpu
from jax.sharding import PartitionSpec as P

F32, BF16 = jnp.float32, jnp.bfloat16
VMEM = pl.BlockSpec(memory_space=pltpu.VMEM)
ANY = pl.BlockSpec(memory_space=pl.ANY)
LIMIT = 40 * 1024 * 1024


def call(body, outs, args, flops=0, after=(), scratch=()):
    moved = sum(a.size * a.dtype.itemsize for a in list(args) + list(outs))
    given, total = len(args), len(args) + len(after)

    def kernel(*refs):
        body(*refs[:given], *refs[total:])

    return pl.pallas_call(
        kernel,
        out_shape=outs,
        in_specs=[VMEM] * given + [ANY] * len(after),
        out_specs=[VMEM] * len(outs),
        scratch_shapes=list(scratch),
        compiler_params=pltpu.CompilerParams(vmem_limit_bytes=LIMIT),
        cost_estimate=pl.CostEstimate(flops=flops, bytes_accessed=moved, transcendentals=0),
    )(*args, *after)


def factors_body(groups, per_device, lam_ref, *refs):
    outs, inv = refs[:-1], refs[-1]
    blocks, modes, cols = inv.shape
    inverse = 1.0 / lam_ref[...]
    for k in range(blocks):
        inv[k] = jnp.broadcast_to(inverse[k : k + 1, :], (cols, modes)).T
    me = lax.axis_index("src")
    for out, group in zip(outs, groups):
        at = 0
        for source, first, count in group:
            start = pl.multiple_of(source(me) * per_device + first, 8)
            for k in range(blocks):
                out[at : at + count] = inv[k, pl.ds(start, count), :]
                at += count


def project_body(count, *refs):
    pieces, (src_ref, mine_ref, theirs_ref) = refs[:count], refs[count:]
    keeps_real = lax.axis_index("space") % 2 == 0
    both = jnp.concatenate([src_ref[0], src_ref[1]], axis=1)
    cols, modes = src_ref.shape[2], pieces[0].shape[2]
    flat = jnp.concatenate([p[...].reshape(-1, p.shape[-1]) for p in pieces], axis=0)
    prod = jnp.dot(flat, both, preferred_element_type=F32).reshape(-1, 2, modes, 2 * cols)
    real = prod[:, 0, :, :cols] + prod[:, 1, :, cols:]
    imag = prod[:, 0, :, cols:] - prod[:, 1, :, :cols]
    mine_ref[...] = jnp.where(keeps_real, real, imag).reshape(mine_ref.shape)
    theirs_ref[...] = jnp.where(keeps_real, imag, real).reshape(theirs_ref.shape)


def sums_body(pairs, *refs):
    for j in range(pairs):
        refs[2 * pairs + j][...] = refs[2 * j][...] + refs[2 * j + 1][...]


def scale_body(one, two, factor, out):
    out[...] = ((one[...] + two[...]) * factor[...]).astype(out.dtype)


def expand_body(counts, first, last, *refs):
    out_ref = refs[-1]
    at = 0 if first else 1
    keeps_real = lax.axis_index("space") % 2 == 0
    left, right = [], []
    for count in counts:
        pieces, (mine_ref, theirs_ref) = refs[at : at + count], refs[at + count : at + count + 2]
        at += count + 2
        row = 0
        for piece in pieces:
            blocks, _, modes, rows = piece.shape
            left.append(piece[...].reshape(blocks * 2 * modes, rows))
            for _ in range(blocks):
                mine, theirs = mine_ref[row : row + modes], theirs_ref[row : row + modes]
                row += modes
                real = jnp.where(keeps_real, mine, theirs)
                imag = jnp.where(keeps_real, theirs, mine)
                right.append(jnp.concatenate([real, imag], axis=1))
                right.append(jnp.concatenate([-imag, real], axis=1))
    left = jnp.concatenate(left, axis=0)
    right = jnp.concatenate(right, axis=0)
    out = lax.dot_general(left, right, (((0,), (0,)), ((), ())), preferred_element_type=F32)
    if not first:
        out = refs[0][...] + out
    if last:
        cols = out_ref.shape[2]
        out_ref[0] = out[:, :cols].astype(out_ref.dtype)
        out_ref[1] = out[:, cols:].astype(out_ref.dtype)
    else:
        out_ref[...] = out


def swap(x, axis, size, bit):
    return lax.ppermute(x, axis, [(i, i ^ bit) for i in range(size)])


def sums(*pairs):
    flat = [v for pair in pairs for v in pair]
    return call(
        functools.partial(sums_body, len(pairs)), [jax.ShapeDtypeStruct(a.shape, F32) for a, _ in pairs], flat
    )


def project(group, sources, n_space, after=()):
    pieces = [piece for piece, _, _ in group]
    _, rows, cols = sources.shape
    height = sum(p.shape[0] * p.shape[2] for p in pieces)
    part = jax.ShapeDtypeStruct((height, cols), F32)
    mine, theirs = call(
        functools.partial(project_body, len(pieces)),
        [part, part],
        pieces + [sources],
        flops=8 * height * rows * cols,
        after=after,
    )
    return mine, swap(theirs, "space", n_space, 1)


def scale(one, two, factor, n_space):
    (mine,) = call(scale_body, [jax.ShapeDtypeStruct(factor.shape, BF16)], [one, two, factor])
    return mine, swap(mine, "space", n_space, 1)


def factors_of(groups, lambdas, per_device, cols):
    blocks = lambdas.shape[0]
    places = [[(source, first, piece.shape[2]) for piece, source, first in group] for group in groups]
    heights = [sum(blocks * count for _, _, count in group) for group in places]
    return call(
        functools.partial(factors_body, places, per_device),
        [jax.ShapeDtypeStruct((height, cols), F32) for height in heights],
        [lambdas],
        scratch=[pltpu.VMEM(lambdas.shape + (cols,), F32)],
    )


def expand(stages, rows, cols):
    acc = None
    for number, stage in enumerate(stages):
        args = [] if acc is None else [acc]
        for group, mine, theirs in stage:
            args += [piece for piece, _, _ in group] + [mine, theirs]
        last = number == len(stages) - 1
        shape = jax.ShapeDtypeStruct((2, rows, cols), BF16) if last else jax.ShapeDtypeStruct((rows, 2 * cols), F32)
        body = functools.partial(expand_body, [len(group) for group, _, _ in stage], acc is None, last)
        (acc,) = call(body, [shape], args, flops=8 * rows * cols * sum(m.shape[0] for _, m, _ in stage))
    return acc


def on_square(vectors, lambdas, sources):
    own = jnp.swapaxes(vectors, 2, 3)
    per_device = own.shape[2]
    _, rows, cols = sources.shape
    half = per_device // 2
    x = functools.partial(swap, axis="src", size=4, bit=1)
    y = functools.partial(swap, axis="src", size=4, bit=2)
    near = functools.partial(swap, axis="space", size=8, bit=2)
    far = functools.partial(swap, axis="space", size=8, bit=4)
    at = lambda bits: lambda me: me ^ bits

    low, high = own[:, :, :half], own[:, :, half:]
    x_low, y_high = x(low), y(high)
    x_high, y_low = x(high), y(low)
    d_low, d_high = y(x_low), x(y_high)
    groups = [
        [(low, at(0), 0), (high, at(0), half), (x_low, at(1), 0), (y_high, at(2), half)],
        [(x_high, at(1), half), (y_low, at(2), 0)],
        [(d_low, at(3), 0), (d_high, at(3), half)],
    ]
    factors = factors_of(groups, lambdas, per_device, cols)

    mine, theirs = project(groups[0], sources, 8)
    (chip0,) = sums((mine, theirs))
    near0 = near(chip0)
    mine, theirs = project(groups[1], sources, 8, after=[chip0])
    (chip1,) = sums((mine, theirs))
    near1 = near(chip1)
    (pair0,) = sums((chip0, near0))
    far0 = far(pair0)
    mine, theirs = project(groups[2], sources, 8, after=[chip1])
    chip2, pair1 = sums((mine, theirs), (chip1, near1))
    near2 = near(chip2)
    far1 = far(pair1)
    (pair2,) = sums((chip2, near2))
    far2 = far(pair2)

    scaled = [
        (group,) + scale(pair, other, factor, 8)
        for group, pair, other, factor in zip(groups, (pair0, pair1, pair2), (far0, far1, far2), factors)
    ]
    return expand([scaled[:2], scaled[2:]], rows, cols)


def on_device(n_src, n_space, vectors, lambdas, sources):
    own = jnp.swapaxes(vectors, 2, 3)
    _, rows, cols = sources.shape
    group = [(own, lambda me: me, 0)]
    for step in range(1, n_src):
        piece = lax.ppermute(own, "src", [(i, (i + step) % n_src) for i in range(n_src)])
        group.append((piece, lambda me, step=step: (me + n_src - step) % n_src, 0))
    (factor,) = factors_of([group], lambdas, own.shape[2], cols)
    mine, theirs = project(group, sources, n_space)
    bit = 2
    while bit < n_space:
        (mine,) = sums((mine, theirs))
        theirs = swap(mine, "space", n_space, bit)
        bit *= 2
    return expand([[(group,) + scale(mine, theirs, factor, n_space)]], rows, cols)


def solution(mesh):
    n_src, n_space = mesh.shape["src"], mesh.shape["space"]
    assert n_space & (n_space - 1) == 0
    square = n_src == 4 and n_space == 8
    return jax.shard_map(
        on_square if square else functools.partial(on_device, n_src, n_space),
        mesh=mesh,
        in_specs=(P(None, None, "space", "src"), P(), P(None, "space", "src")),
        out_specs=P(None, "space", "src"),
        check_vma=False,
    )
```

time: 114 us -> 36 us (0.32)
  waiting for transfers between devices: 55.6 us -> 10.3 us
  blocking collectives: 32.3 us -> 0 us
  starting transfers between devices: 0.01 us -> 21 us
  between operations: 13.6 us -> 0.16 us
  matrix products: 5.97 us -> 0 us
  Pallas kernels: 0 us -> 3.17 us
  other arithmetic: 3.13 us -> 0 us
  local copies, waits for them, and re-layouts: 3.5 us -> 1.15 us
    psum x1 -> x0, waiting for transfers between devices: 55.6 us -> none  [scaled_coeffs(): summed = lax.psum(pair, 'space')]
    all_gather x3 -> x0, blocking collectives: 32.3 us -> none  [on_device(): whole_block = lax.all_gather(vectors[number], 'src', axis=2, tiled=True)]
    ppermute x0 -> x18, starting transfers between devices: none -> 21 us  [swap(): return lax.ppermute(x, axis, [(i, i ^ bit) for i in range(size)])]
    ppermute x0 -> x18, waiting for transfers between devices: none -> 10.3 us  [swap(): return lax.ppermute(x, axis, [(i, i ^ bit) for i in range(size)])]
    dot_general x24 -> x0, matrix products: 5.97 us -> none  [the longest x3 0.78 us: expand(): jnp.dot(vec_im, scaled_re, preferred_element_type=jnp.float32)]
    pallas_call x0 -> x14, Pallas kernels: none -> 3.17 us  [call(): pl.pallas_call(kernel, out_shape=outs, in_specs=[VMEM] * given + [ANY] *...]
    broadcast_in_dim x3 -> x0, other arithmetic: 1.98 us -> none  [on_device(): pair = jnp.stack([partial_re, partial_im])[:, None]]
    unnamed x8 -> x4, local copies, waits for them, and re-layouts: 1.35 us -> 0.01 us
  transfers between devices with their start and end apart: 1 -> 18, of which waited for: 1 -> 8; matrix products, arithmetic and copies ran while one was open for 0% -> 0% of each run, Pallas kernels for 0% -> 5%
where the time goes in v2:
time: 36 us; the launch traced here: 35.8 us
  starting transfers between devices  21 us (58%)
  waiting for transfers between devices  10.3 us (29%)
  Pallas kernels  3.17 us (9%)
  local copies, waits for them, and re-layouts  1.15 us (3%)
    ppermute x18, starting transfers between devices, swap(): return lax.ppermute(x, axis, [(i, i ^ bit) for i in range(size)])  21 us
    ppermute x18, waiting for transfers between devices, swap(): return lax.ppermute(x, axis, [(i, i ^ bit) for i in range(size)])  10.3 us
    pallas_call x14, Pallas kernels, call(): pl.pallas_call(kernel, out_shape=outs, in_specs=[VMEM] * given + [ANY] *...  3.17 us
    slice x1, local copies, waits for them, and re-layouts, on_square(): low, high = (own[:, :, :half], own[:, :, half:])  1.14 us
  transfers between devices with their start and end apart: 18, of which 8 were waited for; matrix products, arithmetic and copies ran while one was open for 0% of the time, Pallas kernels for 5%

profile of v2, /device:TPU:0, one launch (start us, length us, event | category | flops | bytes accessed | tf_op | source)
XLA Modules:
  0.0 35.8 jit_solution(2990540706856222224)
XLA Ops:
  0.0 1.1 %fusion = (bf16[3,2,16,1152]{3,2,1,0:T(8,128)(2,1)S(1)}, bf16[3,2,16,1152]{3,2,1,0:T(8,128)(2,1)S(1)}) fusion(bf16[3,2,32,1152]{3,2,1,0:T(8,128)(2,1)} %bitcast.1), kind=kLoop, calls=%fused_computation | loop fusion | bytes 884736 | tf_op jit(solution)/shard_map/slice | solution.py:171
  1.1 3.0 %collective-permute-start = (bf16[3,2,16,1152]{3,2,1,0:T(8,128)(2,1)S(1)}, bf16[3,2,16,1152]{3,2,1,0:T(8,128)(2,1)S(1)}, u32[]{:S(2)}, u32[]{:S(2)}) collective-permute-start(bf16[3,2,16,1152]{3,2,1,0:T(8,128)(2,1)S(1)} %get-tuple-element.28.refs_0_), channel_id=1, source_target_pairs={{0,8},{8,0},{16,24},{24,16},{1,9},{9,1},{17,25},{25,17},{2,10},{10... | collective-permute-start | bytes 663560 | tf_op jit(solution)/shard_map/ppermute | solution.py:105
  4.2 1.5 %collective-permute-start.1 = (bf16[3,2,16,1152]{3,2,1,0:T(8,128)(2,1)S(1)}, bf16[3,2,16,1152]{3,2,1,0:T(8,128)(2,1)S(1)}, u32[]{:S(2)}, u32[]{:S(2)}) collective-permute-start(bf16[3,2,16,1152]{3,2,1,0:T(8,128)(2,1)S(1)} %get-tuple-element.27.refs_1_), channel_id=1, source_target_pairs={{0,16},{8,24},{16,0},{24,8},{1,17},{9,25},{17,1},{25,9},{2,18},{10... | collective-permute-start | bytes 663560 | tf_op jit(solution)/shard_map/ppermute | solution.py:105
  5.7 0.5 %collective-permute-start.6 = (bf16[3,2,16,1152]{3,2,1,0:T(8,128)(2,1)S(1)}, bf16[3,2,16,1152]{3,2,1,0:T(8,128)(2,1)S(1)}, u32[]{:S(2)}, u32[]{:S(2)}) collective-permute-start(bf16[3,2,16,1152]{3,2,1,0:T(8,128)(2,1)S(1)} %get-tuple-element.27.refs_1_), channel_id=1, source_target_pairs={{0,8},{8,0},{16,24},{24,16},{1,9},{9,1},{17,25},{25,17},{2,10},{10... | collective-permute-start | bytes 663560 | tf_op jit(solution)/shard_map/ppermute | solution.py:105
  6.3 4.2 %collective-permute-done.refs_2_ = bf16[3,2,16,1152]{3,2,1,0:T(8,128)(2,1)S(1)} collective-permute-done((bf16[3,2,16,1152]{3,2,1,0:T(8,128)(2,1)S(1)}, bf16[3,2,16,1152]{3,2,1,0:T(8,128)(2,1)S(1)}, u32[]{:S(2)}, u32[]{:S(2)}) %collective-permute-start) | collective-permute-done | bytes 221216 | tf_op jit(solution)/shard_map/ppermute | solution.py:105
  10.4 2.1 %collective-permute-start.8 = (bf16[3,2,16,1152]{3,2,1,0:T(8,128)(2,1)S(1)}, bf16[3,2,16,1152]{3,2,1,0:T(8,128)(2,1)S(1)}, u32[]{:S(2)}, u32[]{:S(2)}) collective-permute-start(bf16[3,2,16,1152]{3,2,1,0:T(8,128)(2,1)S(1)} %collective-permute-done.refs_2_), channel_id=1, source_target_pairs={{0,16},{8,24},{16,0},{24,8},{1,17},{9,25},{17,1},{25,9},{2,18},{10... | collective-permute-start | bytes 663560 | tf_op jit(solution)/shard_map/ppermute | solution.py:105
  12.5 1.5 %collective-permute-start.9 = (bf16[3,2,16,1152]{3,2,1,0:T(8,128)(2,1)S(1)}, bf16[3,2,16,1152]{3,2,1,0:T(8,128)(2,1)S(1)}, u32[]{:S(2)}, u32[]{:S(2)}) collective-permute-start(bf16[3,2,16,1152]{3,2,1,0:T(8,128)(2,1)S(1)} %collective-permute-done.1.refs_3_), channel_id=1, source_target_pairs={{0,8},{8,0},{16,24},{24,16},{1,9},{9,1},{17,25},{25,17},{2,10},{10... | collective-permute-start | bytes 663560 | tf_op jit(solution)/shard_map/ppermute | solution.py:105
  14.0 0.4 %shard_map.37 = (f32[192,128]{1,0:T(8,128)S(1)}, f32[192,128]{1,0:T(8,128)S(1)}) custom-call(bf16[3,2,16,1152]{3,2,1,0:T(8,128)(2,1)S(1)} %get-tuple-element.28.refs_0_, bf16[3,2,16,1152]{3,2,1,0:T(8,128)(2,1)S(1)} %get-tuple-element.27.refs_1_, bf16[3,2,16,1152]{3,2,1,0:T(8,128)(2,1)S(1)} %collective-permute-done.refs_2_, ...), custom_call_target="tpu_custom_call" | custom-call | flops 226492416 | bytes 1671168 | tf_op jit(solution)/shard_map/pallas_call | solution.py:23
  14.4 0.1 collective-permute-start.2
  14.5 1.3 %collective-permute-done.2.refs_1_ = f32[192,128]{1,0:T(8,128)S(1)} collective-permute-done((f32[192,128]{1,0:T(8,128)S(1)}, f32[192,128]{1,0:T(8,128)S(1)}, u32[]{:S(2)}, u32[]{:S(2)}) %collective-permute-start.2) | collective-permute-done | bytes 98336 | tf_op jit(solution)/shard_map/ppermute | solution.py:105
  15.8 1.6 %collective-permute-start.3 = (f32[192,128]{1,0:T(8,128)S(1)}, f32[192,128]{1,0:T(8,128)S(1)}, u32[]{:S(2)}, u32[]{:S(2)}) collective-permute-start(f32[192,128]{1,0:T(8,128)S(1)} %shard_map.38.refs_0_.refs_3_), channel_id=1, source_target_pairs={{0,2},{1,3},{2,0},{3,1},{4,6},{5,7},{6,4},{7,5},{8,10},{9,11},{10,... | collective-permute-start | bytes 294920 | tf_op jit(solution)/shard_map/ppermute | solution.py:105
  17.5 0.3 shard_map.42
  17.8 0.1 collective-permute-start.10
  17.9 1.2 %collective-permute-done.10.refs_1_ = f32[96,128]{1,0:T(8,128)S(1)} collective-permute-done((f32[96,128]{1,0:T(8,128)S(1)}, f32[96,128]{1,0:T(8,128)S(1)}, u32[]{:S(2)}, u32[]{:S(2)}) %collective-permute-start.10) | collective-permute-done | bytes 49184 | tf_op jit(solution)/shard_map/ppermute | solution.py:105
  19.1 1.4 %collective-permute-start.12 = (f32[96,128]{1,0:T(8,128)S(1)}, f32[96,128]{1,0:T(8,128)S(1)}, u32[]{:S(2)}, u32[]{:S(2)}) collective-permute-start(f32[96,128]{1,0:T(8,128)S(1)} %shard_map.43.refs_3_.refs_2_), channel_id=1, source_target_pairs={{0,2},{1,3},{2,0},{3,1},{4,6},{5,7},{6,4},{7,5},{8,10},{9,11},{10,... | collective-permute-start | bytes 147464 | tf_op jit(solution)/shard_map/ppermute | solution.py:105
  20.5 0.3 shard_map.44
  20.8 0.1 collective-permute-start.11
  20.9 2.7 %collective-permute-start.4 = (f32[192,128]{1,0:T(8,128)S(1)}, f32[192,128]{1,0:T(8,128)S(1)}, u32[]{:S(2)}, u32[]{:S(2)}) collective-permute-start(f32[192,128]{1,0:T(8,128)S(1)} %shard_map.39.refs_0_), channel_id=1, source_target_pairs={{0,4},{1,5},{2,6},{3,7},{4,0},{5,1},{6,2},{7,3},{8,12},{9,13},{10,... | collective-permute-start | bytes 294920 | tf_op jit(solution)/shard_map/ppermute | solution.py:105
  23.6 1.6 %collective-permute-start.15 = (f32[96,128]{1,0:T(8,128)S(1)}, f32[96,128]{1,0:T(8,128)S(1)}, u32[]{:S(2)}, u32[]{:S(2)}) collective-permute-start(f32[96,128]{1,0:T(8,128)S(1)} %get-tuple-element.25.refs_0_), channel_id=1, source_target_pairs={{0,2},{1,3},{2,0},{3,1},{4,6},{5,7},{6,4},{7,5},{8,10},{9,11},{10,... | collective-permute-start | bytes 147464 | tf_op jit(solution)/shard_map/ppermute | solution.py:105
  25.3 2.0 %collective-permute-start.13 = (f32[96,128]{1,0:T(8,128)S(1)}, f32[96,128]{1,0:T(8,128)S(1)}, u32[]{:S(2)}, u32[]{:S(2)}) collective-permute-start(f32[96,128]{1,0:T(8,128)S(1)} %get-tuple-element.23.refs_0_), channel_id=1, source_target_pairs={{0,4},{1,5},{2,6},{3,7},{4,0},{5,1},{6,2},{7,3},{8,12},{9,13},{10,... | collective-permute-start | bytes 147464 | tf_op jit(solution)/shard_map/ppermute | solution.py:105
  27.3 0.1 shard_map.40
  27.4 0.4 collective-permute-done.15.refs_1_
  27.8 2.6 %collective-permute-start.16 = (f32[96,128]{1,0:T(8,128)S(1)}, f32[96,128]{1,0:T(8,128)S(1)}, u32[]{:S(2)}, u32[]{:S(2)}) collective-permute-start(f32[96,128]{1,0:T(8,128)S(1)} %shard_map.48.refs_0_), channel_id=1, source_target_pairs={{0,4},{1,5},{2,6},{3,7},{4,0},{5,1},{6,2},{7,3},{8,12},{9,13},{10,... | collective-permute-start | bytes 147464 | tf_op jit(solution)/shard_map/ppermute | solution.py:105
  30.4 0.3 collective-permute-done.4.refs_1_
  30.7 0.1 collective-permute-start.5
  30.8 0.9 %collective-permute-done.13.refs_1_ = f32[96,128]{1,0:T(8,128)S(1)} collective-permute-done((f32[96,128]{1,0:T(8,128)S(1)}, f32[96,128]{1,0:T(8,128)S(1)}, u32[]{:S(2)}, u32[]{:S(2)}) %collective-permute-start.13) | collective-permute-done | bytes 49184 | tf_op jit(solution)/shard_map/ppermute | solution.py:105
  31.7 0.1 collective-permute-start.14
  31.8 1.6 %collective-permute-done.16.refs_1_ = f32[96,128]{1,0:T(8,128)S(1)} collective-permute-done((f32[96,128]{1,0:T(8,128)S(1)}, f32[96,128]{1,0:T(8,128)S(1)}, u32[]{:S(2)}, u32[]{:S(2)}) %collective-permute-start.16) | collective-permute-done | bytes 49184 | tf_op jit(solution)/shard_map/ppermute | solution.py:105
  33.4 0.1 collective-permute-start.17
  33.5 0.7 %shard_map.47.refs_0_ = f32[1152,256]{1,0:T(8,128)S(1)} custom-call(bf16[3,2,16,1152]{3,2,1,0:T(8,128)(2,1)S(1)} %get-tuple-element.28.refs_0_, bf16[3,2,16,1152]{3,2,1,0:T(8,128)(2,1)S(1)} %get-tuple-element.27.refs_1_, bf16[3,2,16,1152]{3,2,1,0:T(8,128)(2,1)S(1)} %collective-permute-done.refs_2_, ...), custom_call_target="tpu_custom_call" | custom-call | flops 339738624 | bytes 2654208 | tf_op jit(solution)/shard_map/pallas_call | solution.py:23
  34.2 0.5 %collective-permute-done.17.refs_4_ = bf16[96,128]{1,0:T(8,128)(2,1)S(1)} collective-permute-done((bf16[96,128]{1,0:T(8,128)(2,1)S(1)}, bf16[96,128]{1,0:T(8,128)(2,1)S(1)}, u32[]{:S(2)}, u32[]{:S(2)}) %collective-permute-start.17) | collective-permute-done | bytes 24608 | tf_op jit(solution)/shard_map/ppermute | solution.py:105
  34.6 1.2 %shard_map.50 = bf16[2,1152,128]{2,1,0:T(8,128)(2,1)} custom-call(f32[1152,256]{1,0:T(8,128)S(1)} %shard_map.47.refs_0_, bf16[3,2,16,1152]{3,2,1,0:T(8,128)(2,1)S(1)} %collective-permute-done.8.refs_0_.refs_1_, bf16[3,2,16,1152]{3,2,1,0:T(8,128)(2,1)S(1)} %collective-permute-done.9.refs_1_.refs_2_, bf16[96,128]{1,0:T(8,128)(2,1)S(1)} %shard_map.49.refs_3_, ...), custom_call_target="tpu_custom_call" | custom-call | flops 113246208 | bytes 2260992 | tf_op jit(solution)/shard_map/pallas_call | solution.py:23
  (23 shorter events, 0.2 us)
Async XLA Ops:
  0.0 14.0 %copy-start = (bf16[2,1152,128]{2,1,0:T(8,128)(2,1)S(1)}, bf16[2,1152,128]{2,1,0:T(8,128)(2,1)}, u32[]{:S(2)}) copy-start(bf16[2,1152,128]{2,1,0:T(8,128)(2,1)} %refs_2_.3) | copy-start | bytes 1769476
  1.1 9.3 %collective-permute-start = (bf16[3,2,16,1152]{3,2,1,0:T(8,128)(2,1)S(1)}, bf16[3,2,16,1152]{3,2,1,0:T(8,128)(2,1)S(1)}, u32[]{:S(2)}, u32[]{:S(2)}) collective-permute-start(bf16[3,2,16,1152]{3,2,1,0:T(8,128)(2,1)S(1)} %get-tuple-element.28.refs_0_), channel_id=1, source_target_pairs={{0,8},{8,0},{16,24},{24,16},{1,9},{9,1},{17,25},{25,17},{2,10},{10... | collective-permute-start | bytes 663560 | tf_op jit(solution)/shard_map/ppermute | solution.py:105
  4.2 8.4 %collective-permute-start.1 = (bf16[3,2,16,1152]{3,2,1,0:T(8,128)(2,1)S(1)}, bf16[3,2,16,1152]{3,2,1,0:T(8,128)(2,1)S(1)}, u32[]{:S(2)}, u32[]{:S(2)}) collective-permute-start(bf16[3,2,16,1152]{3,2,1,0:T(8,128)(2,1)S(1)} %get-tuple-element.27.refs_1_), channel_id=1, source_target_pairs={{0,16},{8,24},{16,0},{24,8},{1,17},{9,25},{17,1},{25,9},{2,18},{10... | collective-permute-start | bytes 663560 | tf_op jit(solution)/shard_map/ppermute | solution.py:105
  5.7 11.8 %collective-permute-start.6 = (bf16[3,2,16,1152]{3,2,1,0:T(8,128)(2,1)S(1)}, bf16[3,2,16,1152]{3,2,1,0:T(8,128)(2,1)S(1)}, u32[]{:S(2)}, u32[]{:S(2)}) collective-permute-start(bf16[3,2,16,1152]{3,2,1,0:T(8,128)(2,1)S(1)} %get-tuple-element.27.refs_1_), channel_id=1, source_target_pairs={{0,8},{8,0},{16,24},{24,16},{1,9},{9,1},{17,25},{25,17},{2,10},{10... | collective-permute-start | bytes 663560 | tf_op jit(solution)/shard_map/ppermute | solution.py:105
  6.2 11.3 %collective-permute-start.7 = (bf16[3,2,16,1152]{3,2,1,0:T(8,128)(2,1)S(1)}, bf16[3,2,16,1152]{3,2,1,0:T(8,128)(2,1)S(1)}, u32[]{:S(2)}, u32[]{:S(2)}) collective-permute-start(bf16[3,2,16,1152]{3,2,1,0:T(8,128)(2,1)S(1)} %get-tuple-element.28.refs_0_), channel_id=1, source_target_pairs={{0,16},{8,24},{16,0},{24,8},{1,17},{9,25},{17,1},{25,9},{2,18},{10... | collective-permute-start | bytes 663560 | tf_op jit(solution)/shard_map/ppermute | solution.py:105
  10.4 10.1 %collective-permute-start.8 = (bf16[3,2,16,1152]{3,2,1,0:T(8,128)(2,1)S(1)}, bf16[3,2,16,1152]{3,2,1,0:T(8,128)(2,1)S(1)}, u32[]{:S(2)}, u32[]{:S(2)}) collective-permute-start(bf16[3,2,16,1152]{3,2,1,0:T(8,128)(2,1)S(1)} %collective-permute-done.refs_2_), channel_id=1, source_target_pairs={{0,16},{8,24},{16,0},{24,8},{1,17},{9,25},{17,1},{25,9},{2,18},{10... | collective-permute-start | bytes 663560 | tf_op jit(solution)/shard_map/ppermute | solution.py:105
  12.5 8.0 %collective-permute-start.9 = (bf16[3,2,16,1152]{3,2,1,0:T(8,128)(2,1)S(1)}, bf16[3,2,16,1152]{3,2,1,0:T(8,128)(2,1)S(1)}, u32[]{:S(2)}, u32[]{:S(2)}) collective-permute-start(bf16[3,2,16,1152]{3,2,1,0:T(8,128)(2,1)S(1)} %collective-permute-done.1.refs_3_), channel_id=1, source_target_pairs={{0,8},{8,0},{16,24},{24,16},{1,9},{9,1},{17,25},{25,17},{2,10},{10... | collective-permute-start | bytes 663560 | tf_op jit(solution)/shard_map/ppermute | solution.py:105
  14.4 1.4 %collective-permute-start.2 = (f32[192,128]{1,0:T(8,128)S(1)}, f32[192,128]{1,0:T(8,128)S(1)}, u32[]{:S(2)}, u32[]{:S(2)}) collective-permute-start(f32[192,128]{1,0:T(8,128)S(1)} %get-tuple-element.17), channel_id=1, source_target_pairs={{0,1},{1,0},{2,3},{3,2},{4,5},{5,4},{6,7},{7,6},{8,9},{9,8},{10,11... | collective-permute-start | bytes 294920 | tf_op jit(solution)/shard_map/ppermute | solution.py:105
  15.8 11.4 %copy-start.1 = (f32[3,128]{1,0:T(4,128)S(1)}, f32[3,128]{1,0:T(4,128)}, u32[]{:S(2)}) copy-start(f32[3,128]{1,0:T(4,128)} %refs_0_.1) | copy-start | bytes 4612
  15.8 5.1 %collective-permute-start.3 = (f32[192,128]{1,0:T(8,128)S(1)}, f32[192,128]{1,0:T(8,128)S(1)}, u32[]{:S(2)}, u32[]{:S(2)}) collective-permute-start(f32[192,128]{1,0:T(8,128)S(1)} %shard_map.38.refs_0_.refs_3_), channel_id=1, source_target_pairs={{0,2},{1,3},{2,0},{3,1},{4,6},{5,7},{6,4},{7,5},{8,10},{9,11},{10,... | collective-permute-start | bytes 294920 | tf_op jit(solution)/shard_map/ppermute | solution.py:105
  17.8 1.3 %collective-permute-start.10 = (f32[96,128]{1,0:T(8,128)S(1)}, f32[96,128]{1,0:T(8,128)S(1)}, u32[]{:S(2)}, u32[]{:S(2)}) collective-permute-start(f32[96,128]{1,0:T(8,128)S(1)} %get-tuple-element.20), channel_id=1, source_target_pairs={{0,1},{1,0},{2,3},{3,2},{4,5},{5,4},{6,7},{7,6},{8,9},{9,8},{10,11... | collective-permute-start | bytes 147464 | tf_op jit(solution)/shard_map/ppermute | solution.py:105
  19.1 4.5 %collective-permute-start.12 = (f32[96,128]{1,0:T(8,128)S(1)}, f32[96,128]{1,0:T(8,128)S(1)}, u32[]{:S(2)}, u32[]{:S(2)}) collective-permute-start(f32[96,128]{1,0:T(8,128)S(1)} %shard_map.43.refs_3_.refs_2_), channel_id=1, source_target_pairs={{0,2},{1,3},{2,0},{3,1},{4,6},{5,7},{6,4},{7,5},{8,10},{9,11},{10,... | collective-permute-start | bytes 147464 | tf_op jit(solution)/shard_map/ppermute | solution.py:105
  20.8 2.8 %collective-permute-start.11 = (f32[96,128]{1,0:T(8,128)S(1)}, f32[96,128]{1,0:T(8,128)S(1)}, u32[]{:S(2)}, u32[]{:S(2)}) collective-permute-start(f32[96,128]{1,0:T(8,128)S(1)} %get-tuple-element.22), channel_id=1, source_target_pairs={{0,1},{1,0},{2,3},{3,2},{4,5},{5,4},{6,7},{7,6},{8,9},{9,8},{10,11... | collective-permute-start | bytes 147464 | tf_op jit(solution)/shard_map/ppermute | solution.py:105
  20.9 9.7 %collective-permute-start.4 = (f32[192,128]{1,0:T(8,128)S(1)}, f32[192,128]{1,0:T(8,128)S(1)}, u32[]{:S(2)}, u32[]{:S(2)}) collective-permute-start(f32[192,128]{1,0:T(8,128)S(1)} %shard_map.39.refs_0_), channel_id=1, source_target_pairs={{0,4},{1,5},{2,6},{3,7},{4,0},{5,1},{6,2},{7,3},{8,12},{9,13},{10,... | collective-permute-start | bytes 294920 | tf_op jit(solution)/shard_map/ppermute | solution.py:105
  23.6 4.2 %collective-permute-start.15 = (f32[96,128]{1,0:T(8,128)S(1)}, f32[96,128]{1,0:T(8,128)S(1)}, u32[]{:S(2)}, u32[]{:S(2)}) collective-permute-start(f32[96,128]{1,0:T(8,128)S(1)} %get-tuple-element.25.refs_0_), channel_id=1, source_target_pairs={{0,2},{1,3},{2,0},{3,1},{4,6},{5,7},{6,4},{7,5},{8,10},{9,11},{10,... | collective-permute-start | bytes 147464 | tf_op jit(solution)/shard_map/ppermute | solution.py:105
  25.3 6.4 %collective-permute-start.13 = (f32[96,128]{1,0:T(8,128)S(1)}, f32[96,128]{1,0:T(8,128)S(1)}, u32[]{:S(2)}, u32[]{:S(2)}) collective-permute-start(f32[96,128]{1,0:T(8,128)S(1)} %get-tuple-element.23.refs_0_), channel_id=1, source_target_pairs={{0,4},{1,5},{2,6},{3,7},{4,0},{5,1},{6,2},{7,3},{8,12},{9,13},{10,... | collective-permute-start | bytes 147464 | tf_op jit(solution)/shard_map/ppermute | solution.py:105
  27.8 5.6 %collective-permute-start.16 = (f32[96,128]{1,0:T(8,128)S(1)}, f32[96,128]{1,0:T(8,128)S(1)}, u32[]{:S(2)}, u32[]{:S(2)}) collective-permute-start(f32[96,128]{1,0:T(8,128)S(1)} %shard_map.48.refs_0_), channel_id=1, source_target_pairs={{0,4},{1,5},{2,6},{3,7},{4,0},{5,1},{6,2},{7,3},{8,12},{9,13},{10,... | collective-permute-start | bytes 147464 | tf_op jit(solution)/shard_map/ppermute | solution.py:105
  30.7 2.8 %collective-permute-start.5 = (bf16[192,128]{1,0:T(8,128)(2,1)S(1)}, bf16[192,128]{1,0:T(8,128)(2,1)S(1)}, u32[]{:S(2)}, u32[]{:S(2)}) collective-permute-start(bf16[192,128]{1,0:T(8,128)(2,1)S(1)} %shard_map.41.refs_4_), channel_id=1, source_target_pairs={{0,1},{1,0},{2,3},{3,2},{4,5},{5,4},{6,7},{7,6},{8,9},{9,8},{10,11... | collective-permute-start | bytes 147464 | tf_op jit(solution)/shard_map/ppermute | solution.py:105
  31.7 1.7 %collective-permute-start.14 = (bf16[96,128]{1,0:T(8,128)(2,1)S(1)}, bf16[96,128]{1,0:T(8,128)(2,1)S(1)}, u32[]{:S(2)}, u32[]{:S(2)}) collective-permute-start(bf16[96,128]{1,0:T(8,128)(2,1)S(1)} %shard_map.46.refs_8_), channel_id=1, source_target_pairs={{0,1},{1,0},{2,3},{3,2},{4,5},{5,4},{6,7},{7,6},{8,9},{9,8},{10,11... | collective-permute-start | bytes 73736 | tf_op jit(solution)/shard_map/ppermute | solution.py:105
  33.4 1.3 %collective-permute-start.17 = (bf16[96,128]{1,0:T(8,128)(2,1)S(1)}, bf16[96,128]{1,0:T(8,128)(2,1)S(1)}, u32[]{:S(2)}, u32[]{:S(2)}) collective-permute-start(bf16[96,128]{1,0:T(8,128)(2,1)S(1)} %shard_map.49.refs_3_), channel_id=1, source_target_pairs={{0,1},{1,0},{2,3},{3,2},{4,5},{5,4},{6,7},{7,6},{8,9},{9,8},{10,11... | collective-permute-start | bytes 73736 | tf_op jit(solution)/shard_map/ppermute | solution.py:105

commit v3 on v2

--- a/solution.py
+++ b/solution.py
@@ -101,6 +101,51 @@
         out_ref[...] = out
 
 
+def turn_body(*refs):
+    flat = jnp.concatenate([p[...].reshape(-1, p.shape[-1]) for p in refs[:-1]], axis=0)
+    refs[-1][...] = flat.T
+
+
+def finish_body(shapes, chunk, acc, turned, mine_ref, theirs_ref, out, held, sems):
+    keeps_real = lax.axis_index("space") % 2 == 0
+    right, row = [], 0
+    for blocks, modes in shapes:
+        for _ in range(blocks):
+            mine, theirs = mine_ref[row : row + modes], theirs_ref[row : row + modes]
+            row += modes
+            real = jnp.where(keeps_real, mine, theirs)
+            imag = jnp.where(keeps_real, theirs, mine)
+            right.append(jnp.concatenate([real, imag], axis=1))
+            right.append(jnp.concatenate([-imag, real], axis=1))
+    right = jnp.concatenate(right, axis=0)
+    _, rows, cols = held.shape
+    copies = []
+    for number, first in enumerate(range(0, rows, chunk)):
+        some = pl.ds(first, chunk)
+        both = acc[some, :] + jnp.dot(turned[some, :], right, preferred_element_type=F32)
+        for part in range(2):
+            held[part, some, :] = both[:, part * cols : (part + 1) * cols].astype(held.dtype)
+            copy = pltpu.make_async_copy(held.at[part, some], out.at[part, some], sems.at[2 * number + part])
+            copy.start()
+            copies.append(copy)
+    for copy in copies:
+        copy.wait()
+
+
+def finish(acc, group, mine, theirs, turned):
+    rows, cols = acc.shape[0], mine.shape[1]
+    chunk = rows // 3 if rows % 48 == 0 else rows
+    shapes = [(piece.shape[0], piece.shape[2]) for piece, _, _ in group]
+    return pl.pallas_call(
+        functools.partial(finish_body, shapes, chunk),
+        out_shape=jax.ShapeDtypeStruct((2, rows, cols), BF16),
+        in_specs=[VMEM] * 4,
+        out_specs=ANY,
+        scratch_shapes=[pltpu.VMEM((2, rows, cols), BF16), pltpu.SemaphoreType.DMA((2 * (rows // chunk),))],
+        compiler_params=pltpu.CompilerParams(vmem_limit_bytes=LIMIT),
+    )(acc, turned, mine, theirs)
+
+
 def swap(x, axis, size, bit):
     return lax.ppermute(x, axis, [(i, i ^ bit) for i in range(size)])
 
@@ -127,8 +172,8 @@
     return mine, swap(theirs, "space", n_space, 1)
 
 
-def scale(one, two, factor, n_space):
-    (mine,) = call(scale_body, [jax.ShapeDtypeStruct(factor.shape, BF16)], [one, two, factor])
+def scale(one, two, factor, n_space, after=()):
+    (mine,) = call(scale_body, [jax.ShapeDtypeStruct(factor.shape, BF16)], [one, two, factor], after=after)
     return mine, swap(mine, "space", n_space, 1)
 
 
@@ -144,13 +189,13 @@
     )
 
 
-def expand(stages, rows, cols):
+def expand(stages, rows, cols, whole=True):
     acc = None
     for number, stage in enumerate(stages):
         args = [] if acc is None else [acc]
         for group, mine, theirs in stage:
             args += [piece for piece, _, _ in group] + [mine, theirs]
-        last = number == len(stages) - 1
+        last = whole and number == len(stages) - 1
         shape = jax.ShapeDtypeStruct((2, rows, cols), BF16) if last else jax.ShapeDtypeStruct((rows, 2 * cols), F32)
         body = functools.partial(expand_body, [len(group) for group, _, _ in stage], acc is None, last)
         (acc,) = call(body, [shape], args, flops=8 * rows * cols * sum(m.shape[0] for _, m, _ in stage))
@@ -182,23 +227,26 @@
     mine, theirs = project(groups[0], sources, 8)
     (chip0,) = sums((mine, theirs))
     near0 = near(chip0)
-    mine, theirs = project(groups[1], sources, 8, after=[chip0])
+    mine, theirs = project(groups[1], sources, 8)
     (chip1,) = sums((mine, theirs))
     near1 = near(chip1)
     (pair0,) = sums((chip0, near0))
     far0 = far(pair0)
-    mine, theirs = project(groups[2], sources, 8, after=[chip1])
+    mine, theirs = project(groups[2], sources, 8)
     chip2, pair1 = sums((mine, theirs), (chip1, near1))
     near2 = near(chip2)
     far1 = far(pair1)
     (pair2,) = sums((chip2, near2))
     far2 = far(pair2)
 
-    scaled = [
-        (group,) + scale(pair, other, factor, 8)
-        for group, pair, other, factor in zip(groups, (pair0, pair1, pair2), (far0, far1, far2), factors)
-    ]
-    return expand([scaled[:2], scaled[2:]], rows, cols)
+    pieces = [piece for piece, _, _ in groups[2]]
+    wide = 2 * factors[2].shape[0]
+    (turned,) = call(turn_body, [jax.ShapeDtypeStruct((rows, wide), BF16)], pieces, after=[chip2])
+    first = (groups[0],) + scale(pair0, far0, factors[0], 8, after=[turned])
+    second = (groups[1],) + scale(pair1, far1, factors[1], 8)
+    mine, theirs = scale(pair2, far2, factors[2], 8)
+    acc = expand([[first, second]], rows, cols, whole=False)
+    return finish(acc, groups[2], mine, theirs, turned)
 
 
 def on_device(n_src, n_space, vectors, lambdas, sources):

time: 36 us -> 35.9 us (level)
    pallas_call x0 -> x1, Pallas kernels: none -> 1.11 us  [finish(): pl.pallas_call(functools.partial(finish_body, shapes, chunk), out_shape=j...]
    pallas_call x14, Pallas kernels: 3.17 us -> 2.19 us  [call(): pl.pallas_call(kernel, out_shape=outs, in_specs=[VMEM] * given + [ANY] *...]
  transfers between devices with their start and end apart: 18 -> 18, of which waited for: 8 -> 9; matrix products, arithmetic and copies ran while one was open for 0% -> 0% of each run, Pallas kernels for 5% -> 6%
where the time goes in v3:
time: 35.9 us; the launch traced here: 35.8 us
  starting transfers between devices  21 us (58%)
  waiting for transfers between devices  10.2 us (28%)
  Pallas kernels  3.3 us (9%)
  local copies, waits for them, and re-layouts  1.15 us (3%)
    ppermute x18, starting transfers between devices, swap(): return lax.ppermute(x, axis, [(i, i ^ bit) for i in range(size)])  21 us
    ppermute x18, waiting for transfers between devices, swap(): return lax.ppermute(x, axis, [(i, i ^ bit) for i in range(size)])  10.2 us
    pallas_call x14, Pallas kernels, call(): pl.pallas_call(kernel, out_shape=outs, in_specs=[VMEM] * given + [ANY] *...  2.19 us
    slice x1, local copies, waits for them, and re-layouts, on_square(): low, high = (own[:, :, :half], own[:, :, half:])  1.14 us
    pallas_call x1, Pallas kernels, finish(): pl.pallas_call(functools.partial(finish_body, shapes, chunk), out_shape=j...  1.11 us
  transfers between devices with their start and end apart: 18, of which 9 were waited for; matrix products, arithmetic and copies ran while one was open for 0% of the time, Pallas kernels for 6%

profile of v3, /device:TPU:0, one launch (start us, length us, event | category | flops | bytes accessed | tf_op | source)
XLA Modules:
  0.0 35.8 jit_solution(14553857029497163965)
XLA Ops:
  0.0 1.1 %fusion = (bf16[3,2,16,1152]{3,2,1,0:T(8,128)(2,1)S(1)}, bf16[3,2,16,1152]{3,2,1,0:T(8,128)(2,1)S(1)}) fusion(bf16[3,2,32,1152]{3,2,1,0:T(8,128)(2,1)} %bitcast.1), kind=kLoop, calls=%fused_computation | loop fusion | bytes 884736 | tf_op jit(solution)/shard_map/slice | solution.py:216
  1.1 3.0 %collective-permute-start.1 = (bf16[3,2,16,1152]{3,2,1,0:T(8,128)(2,1)S(1)}, bf16[3,2,16,1152]{3,2,1,0:T(8,128)(2,1)S(1)}, u32[]{:S(2)}, u32[]{:S(2)}) collective-permute-start(bf16[3,2,16,1152]{3,2,1,0:T(8,128)(2,1)S(1)} %get-tuple-element.27.refs_1_), channel_id=1, source_target_pairs={{0,16},{8,24},{16,0},{24,8},{1,17},{9,25},{17,1},{25,9},{2,18},{10... | collective-permute-start | bytes 663560 | tf_op jit(solution)/shard_map/ppermute | solution.py:150
  4.2 1.5 %collective-permute-start = (bf16[3,2,16,1152]{3,2,1,0:T(8,128)(2,1)S(1)}, bf16[3,2,16,1152]{3,2,1,0:T(8,128)(2,1)S(1)}, u32[]{:S(2)}, u32[]{:S(2)}) collective-permute-start(bf16[3,2,16,1152]{3,2,1,0:T(8,128)(2,1)S(1)} %get-tuple-element.28.refs_0_), channel_id=1, source_target_pairs={{0,8},{8,0},{16,24},{24,16},{1,9},{9,1},{17,25},{25,17},{2,10},{10... | collective-permute-start | bytes 663560 | tf_op jit(solution)/shard_map/ppermute | solution.py:150
  5.7 0.5 %collective-permute-start.8 = (bf16[3,2,16,1152]{3,2,1,0:T(8,128)(2,1)S(1)}, bf16[3,2,16,1152]{3,2,1,0:T(8,128)(2,1)S(1)}, u32[]{:S(2)}, u32[]{:S(2)}) collective-permute-start(bf16[3,2,16,1152]{3,2,1,0:T(8,128)(2,1)S(1)} %get-tuple-element.27.refs_1_), channel_id=1, source_target_pairs={{0,8},{8,0},{16,24},{24,16},{1,9},{9,1},{17,25},{25,17},{2,10},{10... | collective-permute-start | bytes 663560 | tf_op jit(solution)/shard_map/ppermute | solution.py:150
  6.2 0.1 collective-permute-start.9
  6.3 4.2 %collective-permute-done.1.refs_3_ = bf16[3,2,16,1152]{3,2,1,0:T(8,128)(2,1)S(1)} collective-permute-done((bf16[3,2,16,1152]{3,2,1,0:T(8,128)(2,1)S(1)}, bf16[3,2,16,1152]{3,2,1,0:T(8,128)(2,1)S(1)}, u32[]{:S(2)}, u32[]{:S(2)}) %collective-permute-start.1) | collective-permute-done | bytes 221216 | tf_op jit(solution)/shard_map/ppermute | solution.py:150
  10.4 2.0 %collective-permute-start.6 = (bf16[3,2,16,1152]{3,2,1,0:T(8,128)(2,1)S(1)}, bf16[3,2,16,1152]{3,2,1,0:T(8,128)(2,1)S(1)}, u32[]{:S(2)}, u32[]{:S(2)}) collective-permute-start(bf16[3,2,16,1152]{3,2,1,0:T(8,128)(2,1)S(1)} %collective-permute-done.1.refs_3_), channel_id=1, source_target_pairs={{0,8},{8,0},{16,24},{24,16},{1,9},{9,1},{17,25},{25,17},{2,10},{10... | collective-permute-start | bytes 663560 | tf_op jit(solution)/shard_map/ppermute | solution.py:150
  12.5 1.5 %collective-permute-start.5 = (bf16[3,2,16,1152]{3,2,1,0:T(8,128)(2,1)S(1)}, bf16[3,2,16,1152]{3,2,1,0:T(8,128)(2,1)S(1)}, u32[]{:S(2)}, u32[]{:S(2)}) collective-permute-start(bf16[3,2,16,1152]{3,2,1,0:T(8,128)(2,1)S(1)} %collective-permute-done.refs_2_), channel_id=1, source_target_pairs={{0,16},{8,24},{16,0},{24,8},{1,17},{9,25},{17,1},{25,9},{2,18},{10... | collective-permute-start | bytes 663560 | tf_op jit(solution)/shard_map/ppermute | solution.py:150
  14.0 0.4 %shard_map.37 = (f32[192,128]{1,0:T(8,128)S(1)}, f32[192,128]{1,0:T(8,128)S(1)}) custom-call(bf16[3,2,16,1152]{3,2,1,0:T(8,128)(2,1)S(1)} %get-tuple-element.28.refs_0_, bf16[3,2,16,1152]{3,2,1,0:T(8,128)(2,1)S(1)} %get-tuple-element.27.refs_1_, bf16[3,2,16,1152]{3,2,1,0:T(8,128)(2,1)S(1)} %collective-permute-done.refs_2_, ...), custom_call_target="tpu_custom_call" | custom-call | flops 226492416 | bytes 1671168 | tf_op jit(solution)/shard_map/pallas_call | solution.py:23
  14.4 0.1 collective-permute-start.2
  14.5 1.3 %collective-permute-done.2.refs_1_ = f32[192,128]{1,0:T(8,128)S(1)} collective-permute-done((f32[192,128]{1,0:T(8,128)S(1)}, f32[192,128]{1,0:T(8,128)S(1)}, u32[]{:S(2)}, u32[]{:S(2)}) %collective-permute-start.2) | collective-permute-done | bytes 98336 | tf_op jit(solution)/shard_map/ppermute | solution.py:150
  15.8 1.6 %collective-permute-start.3 = (f32[192,128]{1,0:T(8,128)S(1)}, f32[192,128]{1,0:T(8,128)S(1)}, u32[]{:S(2)}, u32[]{:S(2)}) collective-permute-start(f32[192,128]{1,0:T(8,128)S(1)} %shard_map.38.refs_0_), channel_id=1, source_target_pairs={{0,2},{1,3},{2,0},{3,1},{4,6},{5,7},{6,4},{7,5},{8,10},{9,11},{10,... | collective-permute-start | bytes 294920 | tf_op jit(solution)/shard_map/ppermute | solution.py:150
  17.5 0.3 shard_map.42
  17.8 0.1 collective-permute-start.10
  17.9 1.2 %collective-permute-done.10.refs_1_ = f32[96,128]{1,0:T(8,128)S(1)} collective-permute-done((f32[96,128]{1,0:T(8,128)S(1)}, f32[96,128]{1,0:T(8,128)S(1)}, u32[]{:S(2)}, u32[]{:S(2)}) %collective-permute-start.10) | collective-permute-done | bytes 49184 | tf_op jit(solution)/shard_map/ppermute | solution.py:150
  19.1 1.4 %collective-permute-start.11 = (f32[96,128]{1,0:T(8,128)S(1)}, f32[96,128]{1,0:T(8,128)S(1)}, u32[]{:S(2)}, u32[]{:S(2)}) collective-permute-start(f32[96,128]{1,0:T(8,128)S(1)} %shard_map.43.refs_2_), channel_id=1, source_target_pairs={{0,2},{1,3},{2,0},{3,1},{4,6},{5,7},{6,4},{7,5},{8,10},{9,11},{10,... | collective-permute-start | bytes 147464 | tf_op jit(solution)/shard_map/ppermute | solution.py:150
  20.6 0.3 shard_map.41
  20.9 0.1 collective-permute-start.7
  21.0 2.7 %collective-permute-start.4 = (f32[192,128]{1,0:T(8,128)S(1)}, f32[192,128]{1,0:T(8,128)S(1)}, u32[]{:S(2)}, u32[]{:S(2)}) collective-permute-start(f32[192,128]{1,0:T(8,128)S(1)} %shard_map.39.refs_0_), channel_id=1, source_target_pairs={{0,4},{1,5},{2,6},{3,7},{4,0},{5,1},{6,2},{7,3},{8,12},{9,13},{10,... | collective-permute-start | bytes 294920 | tf_op jit(solution)/shard_map/ppermute | solution.py:150
  23.6 1.6 %collective-permute-start.15 = (f32[96,128]{1,0:T(8,128)S(1)}, f32[96,128]{1,0:T(8,128)S(1)}, u32[]{:S(2)}, u32[]{:S(2)}) collective-permute-start(f32[96,128]{1,0:T(8,128)S(1)} %get-tuple-element.23.refs_2_.refs_0_), channel_id=1, source_target_pairs={{0,2},{1,3},{2,0},{3,1},{4,6},{5,7},{6,4},{7,5},{8,10},{9,11},{10,... | collective-permute-start | bytes 147464 | tf_op jit(solution)/shard_map/ppermute | solution.py:150
  25.3 2.0 %collective-permute-start.13 = (f32[96,128]{1,0:T(8,128)S(1)}, f32[96,128]{1,0:T(8,128)S(1)}, u32[]{:S(2)}, u32[]{:S(2)}) collective-permute-start(f32[96,128]{1,0:T(8,128)S(1)} %get-tuple-element.24.refs_0_), channel_id=1, source_target_pairs={{0,4},{1,5},{2,6},{3,7},{4,0},{5,1},{6,2},{7,3},{8,12},{9,13},{10,... | collective-permute-start | bytes 147464 | tf_op jit(solution)/shard_map/ppermute | solution.py:150
  27.3 0.1 shard_map.40
  27.5 0.2 shard_map.45.refs_3_.turned
  27.7 0.1 collective-permute-done.15.refs_1_
  27.8 2.6 %collective-permute-start.16 = (f32[96,128]{1,0:T(8,128)S(1)}, f32[96,128]{1,0:T(8,128)S(1)}, u32[]{:S(2)}, u32[]{:S(2)}) collective-permute-start(f32[96,128]{1,0:T(8,128)S(1)} %shard_map.49.refs_0_), channel_id=1, source_target_pairs={{0,4},{1,5},{2,6},{3,7},{4,0},{5,1},{6,2},{7,3},{8,12},{9,13},{10,... | collective-permute-start | bytes 147464 | tf_op jit(solution)/shard_map/ppermute | solution.py:150
  30.4 0.3 collective-permute-done.4.refs_1_
  30.8 0.9 %collective-permute-done.13.refs_1_ = f32[96,128]{1,0:T(8,128)S(1)} collective-permute-done((f32[96,128]{1,0:T(8,128)S(1)}, f32[96,128]{1,0:T(8,128)S(1)}, u32[]{:S(2)}, u32[]{:S(2)}) %collective-permute-start.13) | collective-permute-done | bytes 49184 | tf_op jit(solution)/shard_map/ppermute | solution.py:150
  31.8 0.1 collective-permute-start.14
  31.8 1.6 %collective-permute-done.16.refs_1_ = f32[96,128]{1,0:T(8,128)S(1)} collective-permute-done((f32[96,128]{1,0:T(8,128)S(1)}, f32[96,128]{1,0:T(8,128)S(1)}, u32[]{:S(2)}, u32[]{:S(2)}) %collective-permute-start.16) | collective-permute-done | bytes 49184 | tf_op jit(solution)/shard_map/ppermute | solution.py:150
  33.5 0.7 %shard_map.48.acc = f32[1152,256]{1,0:T(8,128)S(1)} custom-call(bf16[3,2,16,1152]{3,2,1,0:T(8,128)(2,1)S(1)} %get-tuple-element.28.refs_0_, bf16[3,2,16,1152]{3,2,1,0:T(8,128)(2,1)S(1)} %get-tuple-element.27.refs_1_, bf16[3,2,16,1152]{3,2,1,0:T(8,128)(2,1)S(1)} %collective-permute-done.refs_2_, bf16[3,2,16,1152]{3,2,1,0:T(8,128)(2,1)S(1)} %collective-permute-done.1.refs_3_, ...), custom_call_target="tpu_custom_call" | custom-call | flops 339738624 | bytes 2654208 | tf_op jit(solution)/shard_map/pallas_call | solution.py:23
  34.2 0.5 %collective-permute-done.17.theirs_ref = bf16[96,128]{1,0:T(8,128)(2,1)S(1)} collective-permute-done((bf16[96,128]{1,0:T(8,128)(2,1)S(1)}, bf16[96,128]{1,0:T(8,128)(2,1)S(1)}, u32[]{:S(2)}, u32[]{:S(2)}) %collective-permute-start.17) | collective-permute-done | bytes 24608 | tf_op jit(solution)/shard_map/ppermute | solution.py:150
  34.7 1.1 %shard_map.51 = bf16[2,1152,128]{2,1,0:T(8,128)(2,1)} custom-call(f32[1152,256]{1,0:T(8,128)S(1)} %shard_map.48.acc, bf16[1152,192]{1,0:T(8,128)(2,1)S(1)} %shard_map.45.refs_3_.turned, bf16[96,128]{1,0:T(8,128)(2,1)S(1)} %shard_map.50.mine_ref, bf16[96,128]{1,0:T(8,128)(2,1)S(1)} %collective-permute-done.17.theirs_ref), custom_call_target="tpu_custom_call" | custom-call | tf_op jit(solution)/shard_map/pallas_call | solution.py:139
  (24 shorter events, 0.4 us)
Async XLA Ops:
  0.0 14.0 %copy-start = (bf16[2,1152,128]{2,1,0:T(8,128)(2,1)S(1)}, bf16[2,1152,128]{2,1,0:T(8,128)(2,1)}, u32[]{:S(2)}) copy-start(bf16[2,1152,128]{2,1,0:T(8,128)(2,1)} %refs_2_.3) | copy-start | bytes 1769476
  1.1 9.3 %collective-permute-start.1 = (bf16[3,2,16,1152]{3,2,1,0:T(8,128)(2,1)S(1)}, bf16[3,2,16,1152]{3,2,1,0:T(8,128)(2,1)S(1)}, u32[]{:S(2)}, u32[]{:S(2)}) collective-permute-start(bf16[3,2,16,1152]{3,2,1,0:T(8,128)(2,1)S(1)} %get-tuple-element.27.refs_1_), channel_id=1, source_target_pairs={{0,16},{8,24},{16,0},{24,8},{1,17},{9,25},{17,1},{25,9},{2,18},{10... | collective-permute-start | bytes 663560 | tf_op jit(solution)/shard_map/ppermute | solution.py:150
  4.2 8.4 %collective-permute-start = (bf16[3,2,16,1152]{3,2,1,0:T(8,128)(2,1)S(1)}, bf16[3,2,16,1152]{3,2,1,0:T(8,128)(2,1)S(1)}, u32[]{:S(2)}, u32[]{:S(2)}) collective-permute-start(bf16[3,2,16,1152]{3,2,1,0:T(8,128)(2,1)S(1)} %get-tuple-element.28.refs_0_), channel_id=1, source_target_pairs={{0,8},{8,0},{16,24},{24,16},{1,9},{9,1},{17,25},{25,17},{2,10},{10... | collective-permute-start | bytes 663560 | tf_op jit(solution)/shard_map/ppermute | solution.py:150
  5.7 11.8 %collective-permute-start.8 = (bf16[3,2,16,1152]{3,2,1,0:T(8,128)(2,1)S(1)}, bf16[3,2,16,1152]{3,2,1,0:T(8,128)(2,1)S(1)}, u32[]{:S(2)}, u32[]{:S(2)}) collective-permute-start(bf16[3,2,16,1152]{3,2,1,0:T(8,128)(2,1)S(1)} %get-tuple-element.27.refs_1_), channel_id=1, source_target_pairs={{0,8},{8,0},{16,24},{24,16},{1,9},{9,1},{17,25},{25,17},{2,10},{10... | collective-permute-start | bytes 663560 | tf_op jit(solution)/shard_map/ppermute | solution.py:150
  6.2 11.3 %collective-permute-start.9 = (bf16[3,2,16,1152]{3,2,1,0:T(8,128)(2,1)S(1)}, bf16[3,2,16,1152]{3,2,1,0:T(8,128)(2,1)S(1)}, u32[]{:S(2)}, u32[]{:S(2)}) collective-permute-start(bf16[3,2,16,1152]{3,2,1,0:T(8,128)(2,1)S(1)} %get-tuple-element.28.refs_0_), channel_id=1, source_target_pairs={{0,16},{8,24},{16,0},{24,8},{1,17},{9,25},{17,1},{25,9},{2,18},{10... | collective-permute-start | bytes 663560 | tf_op jit(solution)/shard_map/ppermute | solution.py:150
  10.4 10.1 %collective-permute-start.6 = (bf16[3,2,16,1152]{3,2,1,0:T(8,128)(2,1)S(1)}, bf16[3,2,16,1152]{3,2,1,0:T(8,128)(2,1)S(1)}, u32[]{:S(2)}, u32[]{:S(2)}) collective-permute-start(bf16[3,2,16,1152]{3,2,1,0:T(8,128)(2,1)S(1)} %collective-permute-done.1.refs_3_), channel_id=1, source_target_pairs={{0,8},{8,0},{16,24},{24,16},{1,9},{9,1},{17,25},{25,17},{2,10},{10... | collective-permute-start | bytes 663560 | tf_op jit(solution)/shard_map/ppermute | solution.py:150
  12.5 8.0 %collective-permute-start.5 = (bf16[3,2,16,1152]{3,2,1,0:T(8,128)(2,1)S(1)}, bf16[3,2,16,1152]{3,2,1,0:T(8,128)(2,1)S(1)}, u32[]{:S(2)}, u32[]{:S(2)}) collective-permute-start(bf16[3,2,16,1152]{3,2,1,0:T(8,128)(2,1)S(1)} %collective-permute-done.refs_2_), channel_id=1, source_target_pairs={{0,16},{8,24},{16,0},{24,8},{1,17},{9,25},{17,1},{25,9},{2,18},{10... | collective-permute-start | bytes 663560 | tf_op jit(solution)/shard_map/ppermute | solution.py:150
  14.4 1.4 %collective-permute-start.2 = (f32[192,128]{1,0:T(8,128)S(1)}, f32[192,128]{1,0:T(8,128)S(1)}, u32[]{:S(2)}, u32[]{:S(2)}) collective-permute-start(f32[192,128]{1,0:T(8,128)S(1)} %get-tuple-element.17), channel_id=1, source_target_pairs={{0,1},{1,0},{2,3},{3,2},{4,5},{5,4},{6,7},{7,6},{8,9},{9,8},{10,11... | collective-permute-start | bytes 294920 | tf_op jit(solution)/shard_map/ppermute | solution.py:150
  15.8 11.5 %copy-start.1 = (f32[3,128]{1,0:T(4,128)S(1)}, f32[3,128]{1,0:T(4,128)}, u32[]{:S(2)}) copy-start(f32[3,128]{1,0:T(4,128)} %refs_0_.1) | copy-start | bytes 4612
  15.8 5.1 %collective-permute-start.3 = (f32[192,128]{1,0:T(8,128)S(1)}, f32[192,128]{1,0:T(8,128)S(1)}, u32[]{:S(2)}, u32[]{:S(2)}) collective-permute-start(f32[192,128]{1,0:T(8,128)S(1)} %shard_map.38.refs_0_), channel_id=1, source_target_pairs={{0,2},{1,3},{2,0},{3,1},{4,6},{5,7},{6,4},{7,5},{8,10},{9,11},{10,... | collective-permute-start | bytes 294920 | tf_op jit(solution)/shard_map/ppermute | solution.py:150
  17.8 1.3 %collective-permute-start.10 = (f32[96,128]{1,0:T(8,128)S(1)}, f32[96,128]{1,0:T(8,128)S(1)}, u32[]{:S(2)}, u32[]{:S(2)}) collective-permute-start(f32[96,128]{1,0:T(8,128)S(1)} %get-tuple-element.22), channel_id=1, source_target_pairs={{0,1},{1,0},{2,3},{3,2},{4,5},{5,4},{6,7},{7,6},{8,9},{9,8},{10,11... | collective-permute-start | bytes 147464 | tf_op jit(solution)/shard_map/ppermute | solution.py:150
  19.1 4.5 %collective-permute-start.11 = (f32[96,128]{1,0:T(8,128)S(1)}, f32[96,128]{1,0:T(8,128)S(1)}, u32[]{:S(2)}, u32[]{:S(2)}) collective-permute-start(f32[96,128]{1,0:T(8,128)S(1)} %shard_map.43.refs_2_), channel_id=1, source_target_pairs={{0,2},{1,3},{2,0},{3,1},{4,6},{5,7},{6,4},{7,5},{8,10},{9,11},{10,... | collective-permute-start | bytes 147464 | tf_op jit(solution)/shard_map/ppermute | solution.py:150
  20.9 2.8 %collective-permute-start.7 = (f32[96,128]{1,0:T(8,128)S(1)}, f32[96,128]{1,0:T(8,128)S(1)}, u32[]{:S(2)}, u32[]{:S(2)}) collective-permute-start(f32[96,128]{1,0:T(8,128)S(1)} %get-tuple-element.20), channel_id=1, source_target_pairs={{0,1},{1,0},{2,3},{3,2},{4,5},{5,4},{6,7},{7,6},{8,9},{9,8},{10,11... | collective-permute-start | bytes 147464 | tf_op jit(solution)/shard_map/ppermute | solution.py:150
  21.0 9.7 %collective-permute-start.4 = (f32[192,128]{1,0:T(8,128)S(1)}, f32[192,128]{1,0:T(8,128)S(1)}, u32[]{:S(2)}, u32[]{:S(2)}) collective-permute-start(f32[192,128]{1,0:T(8,128)S(1)} %shard_map.39.refs_0_), channel_id=1, source_target_pairs={{0,4},{1,5},{2,6},{3,7},{4,0},{5,1},{6,2},{7,3},{8,12},{9,13},{10,... | collective-permute-start | bytes 294920 | tf_op jit(solution)/shard_map/ppermute | solution.py:150
  23.6 4.2 %collective-permute-start.15 = (f32[96,128]{1,0:T(8,128)S(1)}, f32[96,128]{1,0:T(8,128)S(1)}, u32[]{:S(2)}, u32[]{:S(2)}) collective-permute-start(f32[96,128]{1,0:T(8,128)S(1)} %get-tuple-element.23.refs_2_.refs_0_), channel_id=1, source_target_pairs={{0,2},{1,3},{2,0},{3,1},{4,6},{5,7},{6,4},{7,5},{8,10},{9,11},{10,... | collective-permute-start | bytes 147464 | tf_op jit(solution)/shard_map/ppermute | solution.py:150
  25.3 6.4 %collective-permute-start.13 = (f32[96,128]{1,0:T(8,128)S(1)}, f32[96,128]{1,0:T(8,128)S(1)}, u32[]{:S(2)}, u32[]{:S(2)}) collective-permute-start(f32[96,128]{1,0:T(8,128)S(1)} %get-tuple-element.24.refs_0_), channel_id=1, source_target_pairs={{0,4},{1,5},{2,6},{3,7},{4,0},{5,1},{6,2},{7,3},{8,12},{9,13},{10,... | collective-permute-start | bytes 147464 | tf_op jit(solution)/shard_map/ppermute | solution.py:150
  27.8 5.6 %collective-permute-start.16 = (f32[96,128]{1,0:T(8,128)S(1)}, f32[96,128]{1,0:T(8,128)S(1)}, u32[]{:S(2)}, u32[]{:S(2)}) collective-permute-start(f32[96,128]{1,0:T(8,128)S(1)} %shard_map.49.refs_0_), channel_id=1, source_target_pairs={{0,4},{1,5},{2,6},{3,7},{4,0},{5,1},{6,2},{7,3},{8,12},{9,13},{10,... | collective-permute-start | bytes 147464 | tf_op jit(solution)/shard_map/ppermute | solution.py:150
  30.7 2.8 %collective-permute-start.12 = (bf16[192,128]{1,0:T(8,128)(2,1)S(1)}, bf16[192,128]{1,0:T(8,128)(2,1)S(1)}, u32[]{:S(2)}, u32[]{:S(2)}) collective-permute-start(bf16[192,128]{1,0:T(8,128)(2,1)S(1)} %shard_map.46.refs_4_), channel_id=1, source_target_pairs={{0,1},{1,0},{2,3},{3,2},{4,5},{5,4},{6,7},{7,6},{8,9},{9,8},{10,11... | collective-permute-start | bytes 147464 | tf_op jit(solution)/shard_map/ppermute | solution.py:150
  31.8 1.7 %collective-permute-start.14 = (bf16[96,128]{1,0:T(8,128)(2,1)S(1)}, bf16[96,128]{1,0:T(8,128)(2,1)S(1)}, u32[]{:S(2)}, u32[]{:S(2)}) collective-permute-start(bf16[96,128]{1,0:T(8,128)(2,1)S(1)} %shard_map.47.refs_8_), channel_id=1, source_target_pairs={{0,1},{1,0},{2,3},{3,2},{4,5},{5,4},{6,7},{7,6},{8,9},{9,8},{10,11... | collective-permute-start | bytes 73736 | tf_op jit(solution)/shard_map/ppermute | solution.py:150
  33.4 1.3 %collective-permute-start.17 = (bf16[96,128]{1,0:T(8,128)(2,1)S(1)}, bf16[96,128]{1,0:T(8,128)(2,1)S(1)}, u32[]{:S(2)}, u32[]{:S(2)}) collective-permute-start(bf16[96,128]{1,0:T(8,128)(2,1)S(1)} %shard_map.50.mine_ref), channel_id=1, source_target_pairs={{0,1},{1,0},{2,3},{3,2},{4,5},{5,4},{6,7},{7,6},{8,9},{9,8},{10,11... | collective-permute-start | bytes 73736 | tf_op jit(solution)/shard_map/ppermute | solution.py:150

commit v4 on v3

--- a/solution.py
+++ b/solution.py
@@ -245,7 +245,7 @@
     first = (groups[0],) + scale(pair0, far0, factors[0], 8, after=[turned])
     second = (groups[1],) + scale(pair1, far1, factors[1], 8)
     mine, theirs = scale(pair2, far2, factors[2], 8)
-    acc = expand([[first, second]], rows, cols, whole=False)
+    acc = expand([[first], [second]], rows, cols, whole=False)
     return finish(acc, groups[2], mine, theirs, turned)
 
 

time: 35.9 us -> 35.9 us (level)
    pallas_call x14 -> x15, Pallas kernels: 2.19 us -> 2.41 us  [call(): pl.pallas_call(kernel, out_shape=outs, in_specs=[VMEM] * given + [ANY] *...]
  transfers between devices with their start and end apart: 18 -> 18, of which waited for: 9 -> 9; matrix products, arithmetic and copies ran while one was open for 0% -> 0% of each run, Pallas kernels for 6% -> 7%
where the time goes in v4:
time: 35.9 us; the launch traced here: 35.8 us
  starting transfers between devices  21 us (58%)
  waiting for transfers between devices  9.93 us (28%)
  Pallas kernels  3.52 us (10%)
  local copies, waits for them, and re-layouts  1.15 us (3%)
    ppermute x18, starting transfers between devices, swap(): return lax.ppermute(x, axis, [(i, i ^ bit) for i in range(size)])  21 us
    ppermute x18, waiting for transfers between devices, swap(): return lax.ppermute(x, axis, [(i, i ^ bit) for i in range(size)])  9.93 us
    pallas_call x15, Pallas kernels, call(): pl.pallas_call(kernel, out_shape=outs, in_specs=[VMEM] * given + [ANY] *...  2.41 us
    slice x1, local copies, waits for them, and re-layouts, on_square(): low, high = (own[:, :, :half], own[:, :, half:])  1.14 us
    pallas_call x1, Pallas kernels, finish(): pl.pallas_call(functools.partial(finish_body, shapes, chunk), out_shape=j...  1.11 us
  transfers between devices with their start and end apart: 18, of which 9 were waited for; matrix products, arithmetic and copies ran while one was open for 0% of the time, Pallas kernels for 7%

profile of v4, /device:TPU:0, one launch (start us, length us, event | category | flops | bytes accessed | tf_op | source)
XLA Modules:
  0.0 35.8 jit_solution(2003983024166768110)
XLA Ops:
  0.0 1.1 %fusion = (bf16[3,2,16,1152]{3,2,1,0:T(8,128)(2,1)S(1)}, bf16[3,2,16,1152]{3,2,1,0:T(8,128)(2,1)S(1)}) fusion(bf16[3,2,32,1152]{3,2,1,0:T(8,128)(2,1)} %bitcast.1), kind=kLoop, calls=%fused_computation | loop fusion | bytes 884736 | tf_op jit(solution)/shard_map/slice | solution.py:216
  1.1 3.0 %collective-permute-start.1 = (bf16[3,2,16,1152]{3,2,1,0:T(8,128)(2,1)S(1)}, bf16[3,2,16,1152]{3,2,1,0:T(8,128)(2,1)S(1)}, u32[]{:S(2)}, u32[]{:S(2)}) collective-permute-start(bf16[3,2,16,1152]{3,2,1,0:T(8,128)(2,1)S(1)} %get-tuple-element.27.refs_1_), channel_id=1, source_target_pairs={{0,16},{8,24},{16,0},{24,8},{1,17},{9,25},{17,1},{25,9},{2,18},{10... | collective-permute-start | bytes 663560 | tf_op jit(solution)/shard_map/ppermute | solution.py:150
  4.2 1.5 %collective-permute-start = (bf16[3,2,16,1152]{3,2,1,0:T(8,128)(2,1)S(1)}, bf16[3,2,16,1152]{3,2,1,0:T(8,128)(2,1)S(1)}, u32[]{:S(2)}, u32[]{:S(2)}) collective-permute-start(bf16[3,2,16,1152]{3,2,1,0:T(8,128)(2,1)S(1)} %get-tuple-element.28.refs_0_), channel_id=1, source_target_pairs={{0,8},{8,0},{16,24},{24,16},{1,9},{9,1},{17,25},{25,17},{2,10},{10... | collective-permute-start | bytes 663560 | tf_op jit(solution)/shard_map/ppermute | solution.py:150
  5.7 0.5 %collective-permute-start.8 = (bf16[3,2,16,1152]{3,2,1,0:T(8,128)(2,1)S(1)}, bf16[3,2,16,1152]{3,2,1,0:T(8,128)(2,1)S(1)}, u32[]{:S(2)}, u32[]{:S(2)}) collective-permute-start(bf16[3,2,16,1152]{3,2,1,0:T(8,128)(2,1)S(1)} %get-tuple-element.27.refs_1_), channel_id=1, source_target_pairs={{0,8},{8,0},{16,24},{24,16},{1,9},{9,1},{17,25},{25,17},{2,10},{10... | collective-permute-start | bytes 663560 | tf_op jit(solution)/shard_map/ppermute | solution.py:150
  6.2 0.1 collective-permute-start.9
  6.3 4.2 %collective-permute-done.1.refs_3_ = bf16[3,2,16,1152]{3,2,1,0:T(8,128)(2,1)S(1)} collective-permute-done((bf16[3,2,16,1152]{3,2,1,0:T(8,128)(2,1)S(1)}, bf16[3,2,16,1152]{3,2,1,0:T(8,128)(2,1)S(1)}, u32[]{:S(2)}, u32[]{:S(2)}) %collective-permute-start.1) | collective-permute-done | bytes 221216 | tf_op jit(solution)/shard_map/ppermute | solution.py:150
  10.4 2.0 %collective-permute-start.6 = (bf16[3,2,16,1152]{3,2,1,0:T(8,128)(2,1)S(1)}, bf16[3,2,16,1152]{3,2,1,0:T(8,128)(2,1)S(1)}, u32[]{:S(2)}, u32[]{:S(2)}) collective-permute-start(bf16[3,2,16,1152]{3,2,1,0:T(8,128)(2,1)S(1)} %collective-permute-done.1.refs_3_), channel_id=1, source_target_pairs={{0,8},{8,0},{16,24},{24,16},{1,9},{9,1},{17,25},{25,17},{2,10},{10... | collective-permute-start | bytes 663560 | tf_op jit(solution)/shard_map/ppermute | solution.py:150
  12.5 1.5 %collective-permute-start.5 = (bf16[3,2,16,1152]{3,2,1,0:T(8,128)(2,1)S(1)}, bf16[3,2,16,1152]{3,2,1,0:T(8,128)(2,1)S(1)}, u32[]{:S(2)}, u32[]{:S(2)}) collective-permute-start(bf16[3,2,16,1152]{3,2,1,0:T(8,128)(2,1)S(1)} %collective-permute-done.refs_2_), channel_id=1, source_target_pairs={{0,16},{8,24},{16,0},{24,8},{1,17},{9,25},{17,1},{25,9},{2,18},{10... | collective-permute-start | bytes 663560 | tf_op jit(solution)/shard_map/ppermute | solution.py:150
  14.0 0.4 %shard_map.37 = (f32[192,128]{1,0:T(8,128)S(1)}, f32[192,128]{1,0:T(8,128)S(1)}) custom-call(bf16[3,2,16,1152]{3,2,1,0:T(8,128)(2,1)S(1)} %get-tuple-element.28.refs_0_, bf16[3,2,16,1152]{3,2,1,0:T(8,128)(2,1)S(1)} %get-tuple-element.27.refs_1_, bf16[3,2,16,1152]{3,2,1,0:T(8,128)(2,1)S(1)} %collective-permute-done.refs_2_, ...), custom_call_target="tpu_custom_call" | custom-call | flops 226492416 | bytes 1671168 | tf_op jit(solution)/shard_map/pallas_call | solution.py:23
  14.5 1.3 %collective-permute-done.2.refs_1_ = f32[192,128]{1,0:T(8,128)S(1)} collective-permute-done((f32[192,128]{1,0:T(8,128)S(1)}, f32[192,128]{1,0:T(8,128)S(1)}, u32[]{:S(2)}, u32[]{:S(2)}) %collective-permute-start.2) | collective-permute-done | bytes 98336 | tf_op jit(solution)/shard_map/ppermute | solution.py:150
  15.8 1.6 %collective-permute-start.3 = (f32[192,128]{1,0:T(8,128)S(1)}, f32[192,128]{1,0:T(8,128)S(1)}, u32[]{:S(2)}, u32[]{:S(2)}) collective-permute-start(f32[192,128]{1,0:T(8,128)S(1)} %shard_map.38.refs_0_), channel_id=1, source_target_pairs={{0,2},{1,3},{2,0},{3,1},{4,6},{5,7},{6,4},{7,5},{8,10},{9,11},{10,... | collective-permute-start | bytes 294920 | tf_op jit(solution)/shard_map/ppermute | solution.py:150
  17.5 0.3 shard_map.42
  17.9 1.2 %collective-permute-done.10.refs_1_ = f32[96,128]{1,0:T(8,128)S(1)} collective-permute-done((f32[96,128]{1,0:T(8,128)S(1)}, f32[96,128]{1,0:T(8,128)S(1)}, u32[]{:S(2)}, u32[]{:S(2)}) %collective-permute-start.10) | collective-permute-done | bytes 49184 | tf_op jit(solution)/shard_map/ppermute | solution.py:150
  19.1 1.4 %collective-permute-start.11 = (f32[96,128]{1,0:T(8,128)S(1)}, f32[96,128]{1,0:T(8,128)S(1)}, u32[]{:S(2)}, u32[]{:S(2)}) collective-permute-start(f32[96,128]{1,0:T(8,128)S(1)} %shard_map.43.refs_2_), channel_id=1, source_target_pairs={{0,2},{1,3},{2,0},{3,1},{4,6},{5,7},{6,4},{7,5},{8,10},{9,11},{10,... | collective-permute-start | bytes 147464 | tf_op jit(solution)/shard_map/ppermute | solution.py:150
  20.6 0.3 shard_map.41
  20.9 0.1 collective-permute-start.7
  21.0 2.7 %collective-permute-start.4 = (f32[192,128]{1,0:T(8,128)S(1)}, f32[192,128]{1,0:T(8,128)S(1)}, u32[]{:S(2)}, u32[]{:S(2)}) collective-permute-start(f32[192,128]{1,0:T(8,128)S(1)} %shard_map.39.refs_0_), channel_id=1, source_target_pairs={{0,4},{1,5},{2,6},{3,7},{4,0},{5,1},{6,2},{7,3},{8,12},{9,13},{10,... | collective-permute-start | bytes 294920 | tf_op jit(solution)/shard_map/ppermute | solution.py:150
  23.7 1.6 %collective-permute-start.15 = (f32[96,128]{1,0:T(8,128)S(1)}, f32[96,128]{1,0:T(8,128)S(1)}, u32[]{:S(2)}, u32[]{:S(2)}) collective-permute-start(f32[96,128]{1,0:T(8,128)S(1)} %get-tuple-element.23.refs_2_.refs_0_), channel_id=1, source_target_pairs={{0,2},{1,3},{2,0},{3,1},{4,6},{5,7},{6,4},{7,5},{8,10},{9,11},{10,... | collective-permute-start | bytes 147464 | tf_op jit(solution)/shard_map/ppermute | solution.py:150
  25.3 2.0 %collective-permute-start.13 = (f32[96,128]{1,0:T(8,128)S(1)}, f32[96,128]{1,0:T(8,128)S(1)}, u32[]{:S(2)}, u32[]{:S(2)}) collective-permute-start(f32[96,128]{1,0:T(8,128)S(1)} %get-tuple-element.24.refs_0_), channel_id=1, source_target_pairs={{0,4},{1,5},{2,6},{3,7},{4,0},{5,1},{6,2},{7,3},{8,12},{9,13},{10,... | collective-permute-start | bytes 147464 | tf_op jit(solution)/shard_map/ppermute | solution.py:150
  27.3 0.1 shard_map.40
  27.5 0.2 shard_map.45.refs_3_.turned
  27.7 0.1 collective-permute-done.15.refs_1_
  27.8 2.6 %collective-permute-start.16 = (f32[96,128]{1,0:T(8,128)S(1)}, f32[96,128]{1,0:T(8,128)S(1)}, u32[]{:S(2)}, u32[]{:S(2)}) collective-permute-start(f32[96,128]{1,0:T(8,128)S(1)} %shard_map.50.refs_0_), channel_id=1, source_target_pairs={{0,4},{1,5},{2,6},{3,7},{4,0},{5,1},{6,2},{7,3},{8,12},{9,13},{10,... | collective-permute-start | bytes 147464 | tf_op jit(solution)/shard_map/ppermute | solution.py:150
  30.4 0.3 collective-permute-done.4.refs_1_
  30.8 1.0 %collective-permute-done.13.refs_1_ = f32[96,128]{1,0:T(8,128)S(1)} collective-permute-done((f32[96,128]{1,0:T(8,128)S(1)}, f32[96,128]{1,0:T(8,128)S(1)}, u32[]{:S(2)}, u32[]{:S(2)}) %collective-permute-start.13) | collective-permute-done | bytes 49184 | tf_op jit(solution)/shard_map/ppermute | solution.py:150
  31.8 0.1 collective-permute-start.14
  31.8 1.6 %collective-permute-done.16.refs_1_ = f32[96,128]{1,0:T(8,128)S(1)} collective-permute-done((f32[96,128]{1,0:T(8,128)S(1)}, f32[96,128]{1,0:T(8,128)S(1)}, u32[]{:S(2)}, u32[]{:S(2)}) %collective-permute-start.16) | collective-permute-done | bytes 49184 | tf_op jit(solution)/shard_map/ppermute | solution.py:150
  33.4 0.1 collective-permute-start.17
  33.5 0.5 %shard_map.47.refs_0_ = f32[1152,256]{1,0:T(8,128)S(1)} custom-call(bf16[3,2,16,1152]{3,2,1,0:T(8,128)(2,1)S(1)} %get-tuple-element.28.refs_0_, bf16[3,2,16,1152]{3,2,1,0:T(8,128)(2,1)S(1)} %get-tuple-element.27.refs_1_, bf16[3,2,16,1152]{3,2,1,0:T(8,128)(2,1)S(1)} %collective-permute-done.refs_2_, ...), custom_call_target="tpu_custom_call" | custom-call | flops 226492416 | bytes 2162688 | tf_op jit(solution)/shard_map/pallas_call | solution.py:23
  34.0 0.4 %shard_map.49.acc = f32[1152,256]{1,0:T(8,128)S(1)} custom-call(f32[1152,256]{1,0:T(8,128)S(1)} %shard_map.47.refs_0_, bf16[3,2,16,1152]{3,2,1,0:T(8,128)(2,1)S(1)} %collective-permute-done.8.refs_0_.refs_1_, bf16[3,2,16,1152]{3,2,1,0:T(8,128)(2,1)S(1)} %collective-permute-done.9.refs_1_.refs_2_, bf16[96,128]{1,0:T(8,128)(2,1)S(1)} %shard_map.48.refs_3_, ...), custom_call_target="tpu_custom_call" | custom-call | flops 113246208 | bytes 2850816 | tf_op jit(solution)/shard_map/pallas_call | solution.py:23
  34.4 0.2 collective-permute-done.17.theirs_ref
  34.7 1.1 %shard_map.52 = bf16[2,1152,128]{2,1,0:T(8,128)(2,1)} custom-call(f32[1152,256]{1,0:T(8,128)S(1)} %shard_map.49.acc, bf16[1152,192]{1,0:T(8,128)(2,1)S(1)} %shard_map.45.refs_3_.turned, bf16[96,128]{1,0:T(8,128)(2,1)S(1)} %shard_map.51.mine_ref, bf16[96,128]{1,0:T(8,128)(2,1)S(1)} %collective-permute-done.17.theirs_ref), custom_call_target="tpu_custom_call" | custom-call | tf_op jit(solution)/shard_map/pallas_call | solution.py:139
  (25 shorter events, 0.4 us)
Async XLA Ops:
  0.0 14.0 %copy-start = (bf16[2,1152,128]{2,1,0:T(8,128)(2,1)S(1)}, bf16[2,1152,128]{2,1,0:T(8,128)(2,1)}, u32[]{:S(2)}) copy-start(bf16[2,1152,128]{2,1,0:T(8,128)(2,1)} %refs_2_.3) | copy-start | bytes 1769476
  1.1 9.3 %collective-permute-start.1 = (bf16[3,2,16,1152]{3,2,1,0:T(8,128)(2,1)S(1)}, bf16[3,2,16,1152]{3,2,1,0:T(8,128)(2,1)S(1)}, u32[]{:S(2)}, u32[]{:S(2)}) collective-permute-start(bf16[3,2,16,1152]{3,2,1,0:T(8,128)(2,1)S(1)} %get-tuple-element.27.refs_1_), channel_id=1, source_target_pairs={{0,16},{8,24},{16,0},{24,8},{1,17},{9,25},{17,1},{25,9},{2,18},{10... | collective-permute-start | bytes 663560 | tf_op jit(solution)/shard_map/ppermute | solution.py:150
  4.2 8.4 %collective-permute-start = (bf16[3,2,16,1152]{3,2,1,0:T(8,128)(2,1)S(1)}, bf16[3,2,16,1152]{3,2,1,0:T(8,128)(2,1)S(1)}, u32[]{:S(2)}, u32[]{:S(2)}) collective-permute-start(bf16[3,2,16,1152]{3,2,1,0:T(8,128)(2,1)S(1)} %get-tuple-element.28.refs_0_), channel_id=1, source_target_pairs={{0,8},{8,0},{16,24},{24,16},{1,9},{9,1},{17,25},{25,17},{2,10},{10... | collective-permute-start | bytes 663560 | tf_op jit(solution)/shard_map/ppermute | solution.py:150
  5.7 11.8 %collective-permute-start.8 = (bf16[3,2,16,1152]{3,2,1,0:T(8,128)(2,1)S(1)}, bf16[3,2,16,1152]{3,2,1,0:T(8,128)(2,1)S(1)}, u32[]{:S(2)}, u32[]{:S(2)}) collective-permute-start(bf16[3,2,16,1152]{3,2,1,0:T(8,128)(2,1)S(1)} %get-tuple-element.27.refs_1_), channel_id=1, source_target_pairs={{0,8},{8,0},{16,24},{24,16},{1,9},{9,1},{17,25},{25,17},{2,10},{10... | collective-permute-start | bytes 663560 | tf_op jit(solution)/shard_map/ppermute | solution.py:150
  6.2 11.3 %collective-permute-start.9 = (bf16[3,2,16,1152]{3,2,1,0:T(8,128)(2,1)S(1)}, bf16[3,2,16,1152]{3,2,1,0:T(8,128)(2,1)S(1)}, u32[]{:S(2)}, u32[]{:S(2)}) collective-permute-start(bf16[3,2,16,1152]{3,2,1,0:T(8,128)(2,1)S(1)} %get-tuple-element.28.refs_0_), channel_id=1, source_target_pairs={{0,16},{8,24},{16,0},{24,8},{1,17},{9,25},{17,1},{25,9},{2,18},{10... | collective-permute-start | bytes 663560 | tf_op jit(solution)/shard_map/ppermute | solution.py:150
  10.4 10.1 %collective-permute-start.6 = (bf16[3,2,16,1152]{3,2,1,0:T(8,128)(2,1)S(1)}, bf16[3,2,16,1152]{3,2,1,0:T(8,128)(2,1)S(1)}, u32[]{:S(2)}, u32[]{:S(2)}) collective-permute-start(bf16[3,2,16,1152]{3,2,1,0:T(8,128)(2,1)S(1)} %collective-permute-done.1.refs_3_), channel_id=1, source_target_pairs={{0,8},{8,0},{16,24},{24,16},{1,9},{9,1},{17,25},{25,17},{2,10},{10... | collective-permute-start | bytes 663560 | tf_op jit(solution)/shard_map/ppermute | solution.py:150
  12.5 8.0 %collective-permute-start.5 = (bf16[3,2,16,1152]{3,2,1,0:T(8,128)(2,1)S(1)}, bf16[3,2,16,1152]{3,2,1,0:T(8,128)(2,1)S(1)}, u32[]{:S(2)}, u32[]{:S(2)}) collective-permute-start(bf16[3,2,16,1152]{3,2,1,0:T(8,128)(2,1)S(1)} %collective-permute-done.refs_2_), channel_id=1, source_target_pairs={{0,16},{8,24},{16,0},{24,8},{1,17},{9,25},{17,1},{25,9},{2,18},{10... | collective-permute-start | bytes 663560 | tf_op jit(solution)/shard_map/ppermute | solution.py:150
  14.4 1.4 %collective-permute-start.2 = (f32[192,128]{1,0:T(8,128)S(1)}, f32[192,128]{1,0:T(8,128)S(1)}, u32[]{:S(2)}, u32[]{:S(2)}) collective-permute-start(f32[192,128]{1,0:T(8,128)S(1)} %get-tuple-element.17), channel_id=1, source_target_pairs={{0,1},{1,0},{2,3},{3,2},{4,5},{5,4},{6,7},{7,6},{8,9},{9,8},{10,11... | collective-permute-start | bytes 294920 | tf_op jit(solution)/shard_map/ppermute | solution.py:150
  15.8 11.5 %copy-start.1 = (f32[3,128]{1,0:T(4,128)S(1)}, f32[3,128]{1,0:T(4,128)}, u32[]{:S(2)}) copy-start(f32[3,128]{1,0:T(4,128)} %refs_0_.1) | copy-start | bytes 4612
  15.8 5.1 %collective-permute-start.3 = (f32[192,128]{1,0:T(8,128)S(1)}, f32[192,128]{1,0:T(8,128)S(1)}, u32[]{:S(2)}, u32[]{:S(2)}) collective-permute-start(f32[192,128]{1,0:T(8,128)S(1)} %shard_map.38.refs_0_), channel_id=1, source_target_pairs={{0,2},{1,3},{2,0},{3,1},{4,6},{5,7},{6,4},{7,5},{8,10},{9,11},{10,... | collective-permute-start | bytes 294920 | tf_op jit(solution)/shard_map/ppermute | solution.py:150
  17.8 1.3 %collective-permute-start.10 = (f32[96,128]{1,0:T(8,128)S(1)}, f32[96,128]{1,0:T(8,128)S(1)}, u32[]{:S(2)}, u32[]{:S(2)}) collective-permute-start(f32[96,128]{1,0:T(8,128)S(1)} %get-tuple-element.22), channel_id=1, source_target_pairs={{0,1},{1,0},{2,3},{3,2},{4,5},{5,4},{6,7},{7,6},{8,9},{9,8},{10,11... | collective-permute-start | bytes 147464 | tf_op jit(solution)/shard_map/ppermute | solution.py:150
  19.1 4.5 %collective-permute-start.11 = (f32[96,128]{1,0:T(8,128)S(1)}, f32[96,128]{1,0:T(8,128)S(1)}, u32[]{:S(2)}, u32[]{:S(2)}) collective-permute-start(f32[96,128]{1,0:T(8,128)S(1)} %shard_map.43.refs_2_), channel_id=1, source_target_pairs={{0,2},{1,3},{2,0},{3,1},{4,6},{5,7},{6,4},{7,5},{8,10},{9,11},{10,... | collective-permute-start | bytes 147464 | tf_op jit(solution)/shard_map/ppermute | solution.py:150
  20.9 2.8 %collective-permute-start.7 = (f32[96,128]{1,0:T(8,128)S(1)}, f32[96,128]{1,0:T(8,128)S(1)}, u32[]{:S(2)}, u32[]{:S(2)}) collective-permute-start(f32[96,128]{1,0:T(8,128)S(1)} %get-tuple-element.20), channel_id=1, source_target_pairs={{0,1},{1,0},{2,3},{3,2},{4,5},{5,4},{6,7},{7,6},{8,9},{9,8},{10,11... | collective-permute-start | bytes 147464 | tf_op jit(solution)/shard_map/ppermute | solution.py:150
  21.0 9.7 %collective-permute-start.4 = (f32[192,128]{1,0:T(8,128)S(1)}, f32[192,128]{1,0:T(8,128)S(1)}, u32[]{:S(2)}, u32[]{:S(2)}) collective-permute-start(f32[192,128]{1,0:T(8,128)S(1)} %shard_map.39.refs_0_), channel_id=1, source_target_pairs={{0,4},{1,5},{2,6},{3,7},{4,0},{5,1},{6,2},{7,3},{8,12},{9,13},{10,... | collective-permute-start | bytes 294920 | tf_op jit(solution)/shard_map/ppermute | solution.py:150
  23.7 4.2 %collective-permute-start.15 = (f32[96,128]{1,0:T(8,128)S(1)}, f32[96,128]{1,0:T(8,128)S(1)}, u32[]{:S(2)}, u32[]{:S(2)}) collective-permute-start(f32[96,128]{1,0:T(8,128)S(1)} %get-tuple-element.23.refs_2_.refs_0_), channel_id=1, source_target_pairs={{0,2},{1,3},{2,0},{3,1},{4,6},{5,7},{6,4},{7,5},{8,10},{9,11},{10,... | collective-permute-start | bytes 147464 | tf_op jit(solution)/shard_map/ppermute | solution.py:150
  25.3 6.4 %collective-permute-start.13 = (f32[96,128]{1,0:T(8,128)S(1)}, f32[96,128]{1,0:T(8,128)S(1)}, u32[]{:S(2)}, u32[]{:S(2)}) collective-permute-start(f32[96,128]{1,0:T(8,128)S(1)} %get-tuple-element.24.refs_0_), channel_id=1, source_target_pairs={{0,4},{1,5},{2,6},{3,7},{4,0},{5,1},{6,2},{7,3},{8,12},{9,13},{10,... | collective-permute-start | bytes 147464 | tf_op jit(solution)/shard_map/ppermute | solution.py:150
  27.8 5.6 %collective-permute-start.16 = (f32[96,128]{1,0:T(8,128)S(1)}, f32[96,128]{1,0:T(8,128)S(1)}, u32[]{:S(2)}, u32[]{:S(2)}) collective-permute-start(f32[96,128]{1,0:T(8,128)S(1)} %shard_map.50.refs_0_), channel_id=1, source_target_pairs={{0,4},{1,5},{2,6},{3,7},{4,0},{5,1},{6,2},{7,3},{8,12},{9,13},{10,... | collective-permute-start | bytes 147464 | tf_op jit(solution)/shard_map/ppermute | solution.py:150
  30.7 2.8 %collective-permute-start.12 = (bf16[192,128]{1,0:T(8,128)(2,1)S(1)}, bf16[192,128]{1,0:T(8,128)(2,1)S(1)}, u32[]{:S(2)}, u32[]{:S(2)}) collective-permute-start(bf16[192,128]{1,0:T(8,128)(2,1)S(1)} %shard_map.46.refs_4_), channel_id=1, source_target_pairs={{0,1},{1,0},{2,3},{3,2},{4,5},{5,4},{6,7},{7,6},{8,9},{9,8},{10,11... | collective-permute-start | bytes 147464 | tf_op jit(solution)/shard_map/ppermute | solution.py:150
  31.8 2.3 %collective-permute-start.14 = (bf16[96,128]{1,0:T(8,128)(2,1)S(1)}, bf16[96,128]{1,0:T(8,128)(2,1)S(1)}, u32[]{:S(2)}, u32[]{:S(2)}) collective-permute-start(bf16[96,128]{1,0:T(8,128)(2,1)S(1)} %shard_map.48.refs_3_), channel_id=1, source_target_pairs={{0,1},{1,0},{2,3},{3,2},{4,5},{5,4},{6,7},{7,6},{8,9},{9,8},{10,11... | collective-permute-start | bytes 73736 | tf_op jit(solution)/shard_map/ppermute | solution.py:150
  33.4 1.3 %collective-permute-start.17 = (bf16[96,128]{1,0:T(8,128)(2,1)S(1)}, bf16[96,128]{1,0:T(8,128)(2,1)S(1)}, u32[]{:S(2)}, u32[]{:S(2)}) collective-permute-start(bf16[96,128]{1,0:T(8,128)(2,1)S(1)} %shard_map.51.mine_ref), channel_id=1, source_target_pairs={{0,1},{1,0},{2,3},{3,2},{4,5},{5,4},{6,7},{7,6},{8,9},{9,8},{10,11... | collective-permute-start | bytes 73736 | tf_op jit(solution)/shard_map/ppermute | solution.py:150

commit v5 on v3

--- a/solution.py
+++ b/solution.py
@@ -241,7 +241,7 @@
 
     pieces = [piece for piece, _, _ in groups[2]]
     wide = 2 * factors[2].shape[0]
-    (turned,) = call(turn_body, [jax.ShapeDtypeStruct((rows, wide), BF16)], pieces, after=[chip2])
+    (turned,) = call(turn_body, [jax.ShapeDtypeStruct((rows, wide), BF16)], pieces, after=[pair2])
     first = (groups[0],) + scale(pair0, far0, factors[0], 8, after=[turned])
     second = (groups[1],) + scale(pair1, far1, factors[1], 8)
     mine, theirs = scale(pair2, far2, factors[2], 8)

time: 35.9 us -> 35.9 us (level)
  no operation moved by 1% of the time
where the time goes in v5:
time: 35.9 us; the launch traced here: 35.8 us
  starting transfers between devices  21 us (58%)
  waiting for transfers between devices  10.2 us (28%)
  Pallas kernels  3.3 us (9%)
  local copies, waits for them, and re-layouts  1.15 us (3%)
    ppermute x18, starting transfers between devices, swap(): return lax.ppermute(x, axis, [(i, i ^ bit) for i in range(size)])  21 us
    ppermute x18, waiting for transfers between devices, swap(): return lax.ppermute(x, axis, [(i, i ^ bit) for i in range(size)])  10.2 us
    pallas_call x14, Pallas kernels, call(): pl.pallas_call(kernel, out_shape=outs, in_specs=[VMEM] * given + [ANY] *...  2.19 us
    slice x1, local copies, waits for them, and re-layouts, on_square(): low, high = (own[:, :, :half], own[:, :, half:])  1.14 us
    pallas_call x1, Pallas kernels, finish(): pl.pallas_call(functools.partial(finish_body, shapes, chunk), out_shape=j...  1.11 us
  transfers between devices with their start and end apart: 18, of which 9 were waited for; matrix products, arithmetic and copies ran while one was open for 0% of the time, Pallas kernels for 6%

profile of v5, /device:TPU:0, one launch (start us, length us, event | category | flops | bytes accessed | tf_op | source)
XLA Modules:
  0.0 35.8 jit_solution(12315519639095754999)
XLA Ops:
  0.0 1.1 %fusion = (bf16[3,2,16,1152]{3,2,1,0:T(8,128)(2,1)S(1)}, bf16[3,2,16,1152]{3,2,1,0:T(8,128)(2,1)S(1)}) fusion(bf16[3,2,32,1152]{3,2,1,0:T(8,128)(2,1)} %bitcast.1), kind=kLoop, calls=%fused_computation | loop fusion | bytes 884736 | tf_op jit(solution)/shard_map/slice | solution.py:216
  1.1 3.0 %collective-permute-start.1 = (bf16[3,2,16,1152]{3,2,1,0:T(8,128)(2,1)S(1)}, bf16[3,2,16,1152]{3,2,1,0:T(8,128)(2,1)S(1)}, u32[]{:S(2)}, u32[]{:S(2)}) collective-permute-start(bf16[3,2,16,1152]{3,2,1,0:T(8,128)(2,1)S(1)} %get-tuple-element.27.refs_1_), channel_id=1, source_target_pairs={{0,16},{8,24},{16,0},{24,8},{1,17},{9,25},{17,1},{25,9},{2,18},{10... | collective-permute-start | bytes 663560 | tf_op jit(solution)/shard_map/ppermute | solution.py:150
  4.2 1.5 %collective-permute-start = (bf16[3,2,16,1152]{3,2,1,0:T(8,128)(2,1)S(1)}, bf16[3,2,16,1152]{3,2,1,0:T(8,128)(2,1)S(1)}, u32[]{:S(2)}, u32[]{:S(2)}) collective-permute-start(bf16[3,2,16,1152]{3,2,1,0:T(8,128)(2,1)S(1)} %get-tuple-element.28.refs_0_), channel_id=1, source_target_pairs={{0,8},{8,0},{16,24},{24,16},{1,9},{9,1},{17,25},{25,17},{2,10},{10... | collective-permute-start | bytes 663560 | tf_op jit(solution)/shard_map/ppermute | solution.py:150
  5.7 0.5 %collective-permute-start.8 = (bf16[3,2,16,1152]{3,2,1,0:T(8,128)(2,1)S(1)}, bf16[3,2,16,1152]{3,2,1,0:T(8,128)(2,1)S(1)}, u32[]{:S(2)}, u32[]{:S(2)}) collective-permute-start(bf16[3,2,16,1152]{3,2,1,0:T(8,128)(2,1)S(1)} %get-tuple-element.27.refs_1_), channel_id=1, source_target_pairs={{0,8},{8,0},{16,24},{24,16},{1,9},{9,1},{17,25},{25,17},{2,10},{10... | collective-permute-start | bytes 663560 | tf_op jit(solution)/shard_map/ppermute | solution.py:150
  6.2 0.1 collective-permute-start.9
  6.3 4.2 %collective-permute-done.1.refs_3_ = bf16[3,2,16,1152]{3,2,1,0:T(8,128)(2,1)S(1)} collective-permute-done((bf16[3,2,16,1152]{3,2,1,0:T(8,128)(2,1)S(1)}, bf16[3,2,16,1152]{3,2,1,0:T(8,128)(2,1)S(1)}, u32[]{:S(2)}, u32[]{:S(2)}) %collective-permute-start.1) | collective-permute-done | bytes 221216 | tf_op jit(solution)/shard_map/ppermute | solution.py:150
  10.4 2.0 %collective-permute-start.6 = (bf16[3,2,16,1152]{3,2,1,0:T(8,128)(2,1)S(1)}, bf16[3,2,16,1152]{3,2,1,0:T(8,128)(2,1)S(1)}, u32[]{:S(2)}, u32[]{:S(2)}) collective-permute-start(bf16[3,2,16,1152]{3,2,1,0:T(8,128)(2,1)S(1)} %collective-permute-done.1.refs_3_), channel_id=1, source_target_pairs={{0,8},{8,0},{16,24},{24,16},{1,9},{9,1},{17,25},{25,17},{2,10},{10... | collective-permute-start | bytes 663560 | tf_op jit(solution)/shard_map/ppermute | solution.py:150
  12.5 1.5 %collective-permute-start.5 = (bf16[3,2,16,1152]{3,2,1,0:T(8,128)(2,1)S(1)}, bf16[3,2,16,1152]{3,2,1,0:T(8,128)(2,1)S(1)}, u32[]{:S(2)}, u32[]{:S(2)}) collective-permute-start(bf16[3,2,16,1152]{3,2,1,0:T(8,128)(2,1)S(1)} %collective-permute-done.refs_2_), channel_id=1, source_target_pairs={{0,16},{8,24},{16,0},{24,8},{1,17},{9,25},{17,1},{25,9},{2,18},{10... | collective-permute-start | bytes 663560 | tf_op jit(solution)/shard_map/ppermute | solution.py:150
  14.0 0.4 %shard_map.37 = (f32[192,128]{1,0:T(8,128)S(1)}, f32[192,128]{1,0:T(8,128)S(1)}) custom-call(bf16[3,2,16,1152]{3,2,1,0:T(8,128)(2,1)S(1)} %get-tuple-element.28.refs_0_, bf16[3,2,16,1152]{3,2,1,0:T(8,128)(2,1)S(1)} %get-tuple-element.27.refs_1_, bf16[3,2,16,1152]{3,2,1,0:T(8,128)(2,1)S(1)} %collective-permute-done.refs_2_, ...), custom_call_target="tpu_custom_call" | custom-call | flops 226492416 | bytes 1671168 | tf_op jit(solution)/shard_map/pallas_call | solution.py:23
  14.4 0.1 collective-permute-start.2
  14.5 1.3 %collective-permute-done.2.refs_1_ = f32[192,128]{1,0:T(8,128)S(1)} collective-permute-done((f32[192,128]{1,0:T(8,128)S(1)}, f32[192,128]{1,0:T(8,128)S(1)}, u32[]{:S(2)}, u32[]{:S(2)}) %collective-permute-start.2) | collective-permute-done | bytes 98336 | tf_op jit(solution)/shard_map/ppermute | solution.py:150
  15.8 1.6 %collective-permute-start.3 = (f32[192,128]{1,0:T(8,128)S(1)}, f32[192,128]{1,0:T(8,128)S(1)}, u32[]{:S(2)}, u32[]{:S(2)}) collective-permute-start(f32[192,128]{1,0:T(8,128)S(1)} %shard_map.38.refs_0_), channel_id=1, source_target_pairs={{0,2},{1,3},{2,0},{3,1},{4,6},{5,7},{6,4},{7,5},{8,10},{9,11},{10,... | collective-permute-start | bytes 294920 | tf_op jit(solution)/shard_map/ppermute | solution.py:150
  17.5 0.3 shard_map.42
  17.8 0.1 collective-permute-start.10
  17.9 1.2 %collective-permute-done.10.refs_1_ = f32[96,128]{1,0:T(8,128)S(1)} collective-permute-done((f32[96,128]{1,0:T(8,128)S(1)}, f32[96,128]{1,0:T(8,128)S(1)}, u32[]{:S(2)}, u32[]{:S(2)}) %collective-permute-start.10) | collective-permute-done | bytes 49184 | tf_op jit(solution)/shard_map/ppermute | solution.py:150
  19.1 1.4 %collective-permute-start.11 = (f32[96,128]{1,0:T(8,128)S(1)}, f32[96,128]{1,0:T(8,128)S(1)}, u32[]{:S(2)}, u32[]{:S(2)}) collective-permute-start(f32[96,128]{1,0:T(8,128)S(1)} %shard_map.43.refs_2_), channel_id=1, source_target_pairs={{0,2},{1,3},{2,0},{3,1},{4,6},{5,7},{6,4},{7,5},{8,10},{9,11},{10,... | collective-permute-start | bytes 147464 | tf_op jit(solution)/shard_map/ppermute | solution.py:150
  20.6 0.3 shard_map.41
  20.9 0.1 collective-permute-start.7
  21.0 2.7 %collective-permute-start.4 = (f32[192,128]{1,0:T(8,128)S(1)}, f32[192,128]{1,0:T(8,128)S(1)}, u32[]{:S(2)}, u32[]{:S(2)}) collective-permute-start(f32[192,128]{1,0:T(8,128)S(1)} %shard_map.39.refs_0_), channel_id=1, source_target_pairs={{0,4},{1,5},{2,6},{3,7},{4,0},{5,1},{6,2},{7,3},{8,12},{9,13},{10,... | collective-permute-start | bytes 294920 | tf_op jit(solution)/shard_map/ppermute | solution.py:150
  23.6 1.6 %collective-permute-start.12 = (f32[96,128]{1,0:T(8,128)S(1)}, f32[96,128]{1,0:T(8,128)S(1)}, u32[]{:S(2)}, u32[]{:S(2)}) collective-permute-start(f32[96,128]{1,0:T(8,128)S(1)} %get-tuple-element.23.refs_0_), channel_id=1, source_target_pairs={{0,2},{1,3},{2,0},{3,1},{4,6},{5,7},{6,4},{7,5},{8,10},{9,11},{10,... | collective-permute-start | bytes 147464 | tf_op jit(solution)/shard_map/ppermute | solution.py:150
  25.3 2.0 %collective-permute-start.14 = (f32[96,128]{1,0:T(8,128)S(1)}, f32[96,128]{1,0:T(8,128)S(1)}, u32[]{:S(2)}, u32[]{:S(2)}) collective-permute-start(f32[96,128]{1,0:T(8,128)S(1)} %get-tuple-element.24.refs_0_), channel_id=1, source_target_pairs={{0,4},{1,5},{2,6},{3,7},{4,0},{5,1},{6,2},{7,3},{8,12},{9,13},{10,... | collective-permute-start | bytes 147464 | tf_op jit(solution)/shard_map/ppermute | solution.py:150
  27.3 0.1 shard_map.40
  27.5 0.3 collective-permute-done.12.refs_1_
  27.8 2.6 %collective-permute-start.16 = (f32[96,128]{1,0:T(8,128)S(1)}, f32[96,128]{1,0:T(8,128)S(1)}, u32[]{:S(2)}, u32[]{:S(2)}) collective-permute-start(f32[96,128]{1,0:T(8,128)S(1)} %shard_map.45.refs_2_.refs_0_), channel_id=1, source_target_pairs={{0,4},{1,5},{2,6},{3,7},{4,0},{5,1},{6,2},{7,3},{8,12},{9,13},{10,... | collective-permute-start | bytes 147464 | tf_op jit(solution)/shard_map/ppermute | solution.py:150
  30.4 0.2 shard_map.46.refs_3_.turned
  30.6 0.1 collective-permute-done.4.refs_1_
  30.8 0.9 %collective-permute-done.14.refs_1_ = f32[96,128]{1,0:T(8,128)S(1)} collective-permute-done((f32[96,128]{1,0:T(8,128)S(1)}, f32[96,128]{1,0:T(8,128)S(1)}, u32[]{:S(2)}, u32[]{:S(2)}) %collective-permute-start.14) | collective-permute-done | bytes 49184 | tf_op jit(solution)/shard_map/ppermute | solution.py:150
  31.8 0.1 collective-permute-start.15
  31.8 1.6 %collective-permute-done.16.refs_1_ = f32[96,128]{1,0:T(8,128)S(1)} collective-permute-done((f32[96,128]{1,0:T(8,128)S(1)}, f32[96,128]{1,0:T(8,128)S(1)}, u32[]{:S(2)}, u32[]{:S(2)}) %collective-permute-start.16) | collective-permute-done | bytes 49184 | tf_op jit(solution)/shard_map/ppermute | solution.py:150
  33.5 0.7 %shard_map.49.acc = f32[1152,256]{1,0:T(8,128)S(1)} custom-call(bf16[3,2,16,1152]{3,2,1,0:T(8,128)(2,1)S(1)} %get-tuple-element.28.refs_0_, bf16[3,2,16,1152]{3,2,1,0:T(8,128)(2,1)S(1)} %get-tuple-element.27.refs_1_, bf16[3,2,16,1152]{3,2,1,0:T(8,128)(2,1)S(1)} %collective-permute-done.refs_2_, bf16[3,2,16,1152]{3,2,1,0:T(8,128)(2,1)S(1)} %collective-permute-done.1.refs_3_, ...), custom_call_target="tpu_custom_call" | custom-call | flops 339738624 | bytes 2654208 | tf_op jit(solution)/shard_map/pallas_call | solution.py:23
  34.2 0.5 %collective-permute-done.17.theirs_ref = bf16[96,128]{1,0:T(8,128)(2,1)S(1)} collective-permute-done((bf16[96,128]{1,0:T(8,128)(2,1)S(1)}, bf16[96,128]{1,0:T(8,128)(2,1)S(1)}, u32[]{:S(2)}, u32[]{:S(2)}) %collective-permute-start.17) | collective-permute-done | bytes 24608 | tf_op jit(solution)/shard_map/ppermute | solution.py:150
  34.7 1.1 %shard_map.51 = bf16[2,1152,128]{2,1,0:T(8,128)(2,1)} custom-call(f32[1152,256]{1,0:T(8,128)S(1)} %shard_map.49.acc, bf16[1152,192]{1,0:T(8,128)(2,1)S(1)} %shard_map.46.refs_3_.turned, bf16[96,128]{1,0:T(8,128)(2,1)S(1)} %shard_map.50.mine_ref, bf16[96,128]{1,0:T(8,128)(2,1)S(1)} %collective-permute-done.17.theirs_ref), custom_call_target="tpu_custom_call" | custom-call | tf_op jit(solution)/shard_map/pallas_call | solution.py:139
  (24 shorter events, 0.4 us)
Async XLA Ops:
  0.0 14.0 %copy-start = (bf16[2,1152,128]{2,1,0:T(8,128)(2,1)S(1)}, bf16[2,1152,128]{2,1,0:T(8,128)(2,1)}, u32[]{:S(2)}) copy-start(bf16[2,1152,128]{2,1,0:T(8,128)(2,1)} %refs_2_.3) | copy-start | bytes 1769476
  1.1 9.3 %collective-permute-start.1 = (bf16[3,2,16,1152]{3,2,1,0:T(8,128)(2,1)S(1)}, bf16[3,2,16,1152]{3,2,1,0:T(8,128)(2,1)S(1)}, u32[]{:S(2)}, u32[]{:S(2)}) collective-permute-start(bf16[3,2,16,1152]{3,2,1,0:T(8,128)(2,1)S(1)} %get-tuple-element.27.refs_1_), channel_id=1, source_target_pairs={{0,16},{8,24},{16,0},{24,8},{1,17},{9,25},{17,1},{25,9},{2,18},{10... | collective-permute-start | bytes 663560 | tf_op jit(solution)/shard_map/ppermute | solution.py:150
  4.2 8.4 %collective-permute-start = (bf16[3,2,16,1152]{3,2,1,0:T(8,128)(2,1)S(1)}, bf16[3,2,16,1152]{3,2,1,0:T(8,128)(2,1)S(1)}, u32[]{:S(2)}, u32[]{:S(2)}) collective-permute-start(bf16[3,2,16,1152]{3,2,1,0:T(8,128)(2,1)S(1)} %get-tuple-element.28.refs_0_), channel_id=1, source_target_pairs={{0,8},{8,0},{16,24},{24,16},{1,9},{9,1},{17,25},{25,17},{2,10},{10... | collective-permute-start | bytes 663560 | tf_op jit(solution)/shard_map/ppermute | solution.py:150
  5.7 11.8 %collective-permute-start.8 = (bf16[3,2,16,1152]{3,2,1,0:T(8,128)(2,1)S(1)}, bf16[3,2,16,1152]{3,2,1,0:T(8,128)(2,1)S(1)}, u32[]{:S(2)}, u32[]{:S(2)}) collective-permute-start(bf16[3,2,16,1152]{3,2,1,0:T(8,128)(2,1)S(1)} %get-tuple-element.27.refs_1_), channel_id=1, source_target_pairs={{0,8},{8,0},{16,24},{24,16},{1,9},{9,1},{17,25},{25,17},{2,10},{10... | collective-permute-start | bytes 663560 | tf_op jit(solution)/shard_map/ppermute | solution.py:150
  6.2 11.3 %collective-permute-start.9 = (bf16[3,2,16,1152]{3,2,1,0:T(8,128)(2,1)S(1)}, bf16[3,2,16,1152]{3,2,1,0:T(8,128)(2,1)S(1)}, u32[]{:S(2)}, u32[]{:S(2)}) collective-permute-start(bf16[3,2,16,1152]{3,2,1,0:T(8,128)(2,1)S(1)} %get-tuple-element.28.refs_0_), channel_id=1, source_target_pairs={{0,16},{8,24},{16,0},{24,8},{1,17},{9,25},{17,1},{25,9},{2,18},{10... | collective-permute-start | bytes 663560 | tf_op jit(solution)/shard_map/ppermute | solution.py:150
  10.4 10.1 %collective-permute-start.6 = (bf16[3,2,16,1152]{3,2,1,0:T(8,128)(2,1)S(1)}, bf16[3,2,16,1152]{3,2,1,0:T(8,128)(2,1)S(1)}, u32[]{:S(2)}, u32[]{:S(2)}) collective-permute-start(bf16[3,2,16,1152]{3,2,1,0:T(8,128)(2,1)S(1)} %collective-permute-done.1.refs_3_), channel_id=1, source_target_pairs={{0,8},{8,0},{16,24},{24,16},{1,9},{9,1},{17,25},{25,17},{2,10},{10... | collective-permute-start | bytes 663560 | tf_op jit(solution)/shard_map/ppermute | solution.py:150
  12.5 8.0 %collective-permute-start.5 = (bf16[3,2,16,1152]{3,2,1,0:T(8,128)(2,1)S(1)}, bf16[3,2,16,1152]{3,2,1,0:T(8,128)(2,1)S(1)}, u32[]{:S(2)}, u32[]{:S(2)}) collective-permute-start(bf16[3,2,16,1152]{3,2,1,0:T(8,128)(2,1)S(1)} %collective-permute-done.refs_2_), channel_id=1, source_target_pairs={{0,16},{8,24},{16,0},{24,8},{1,17},{9,25},{17,1},{25,9},{2,18},{10... | collective-permute-start | bytes 663560 | tf_op jit(solution)/shard_map/ppermute | solution.py:150
  14.4 1.4 %collective-permute-start.2 = (f32[192,128]{1,0:T(8,128)S(1)}, f32[192,128]{1,0:T(8,128)S(1)}, u32[]{:S(2)}, u32[]{:S(2)}) collective-permute-start(f32[192,128]{1,0:T(8,128)S(1)} %get-tuple-element.17), channel_id=1, source_target_pairs={{0,1},{1,0},{2,3},{3,2},{4,5},{5,4},{6,7},{7,6},{8,9},{9,8},{10,11... | collective-permute-start | bytes 294920 | tf_op jit(solution)/shard_map/ppermute | solution.py:150
  15.8 11.5 %copy-start.1 = (f32[3,128]{1,0:T(4,128)S(1)}, f32[3,128]{1,0:T(4,128)}, u32[]{:S(2)}) copy-start(f32[3,128]{1,0:T(4,128)} %refs_0_.1) | copy-start | bytes 4612
  15.8 5.1 %collective-permute-start.3 = (f32[192,128]{1,0:T(8,128)S(1)}, f32[192,128]{1,0:T(8,128)S(1)}, u32[]{:S(2)}, u32[]{:S(2)}) collective-permute-start(f32[192,128]{1,0:T(8,128)S(1)} %shard_map.38.refs_0_), channel_id=1, source_target_pairs={{0,2},{1,3},{2,0},{3,1},{4,6},{5,7},{6,4},{7,5},{8,10},{9,11},{10,... | collective-permute-start | bytes 294920 | tf_op jit(solution)/shard_map/ppermute | solution.py:150
  17.8 1.3 %collective-permute-start.10 = (f32[96,128]{1,0:T(8,128)S(1)}, f32[96,128]{1,0:T(8,128)S(1)}, u32[]{:S(2)}, u32[]{:S(2)}) collective-permute-start(f32[96,128]{1,0:T(8,128)S(1)} %get-tuple-element.22), channel_id=1, source_target_pairs={{0,1},{1,0},{2,3},{3,2},{4,5},{5,4},{6,7},{7,6},{8,9},{9,8},{10,11... | collective-permute-start | bytes 147464 | tf_op jit(solution)/shard_map/ppermute | solution.py:150
  19.1 4.5 %collective-permute-start.11 = (f32[96,128]{1,0:T(8,128)S(1)}, f32[96,128]{1,0:T(8,128)S(1)}, u32[]{:S(2)}, u32[]{:S(2)}) collective-permute-start(f32[96,128]{1,0:T(8,128)S(1)} %shard_map.43.refs_2_), channel_id=1, source_target_pairs={{0,2},{1,3},{2,0},{3,1},{4,6},{5,7},{6,4},{7,5},{8,10},{9,11},{10,... | collective-permute-start | bytes 147464 | tf_op jit(solution)/shard_map/ppermute | solution.py:150
  20.9 2.8 %collective-permute-start.7 = (f32[96,128]{1,0:T(8,128)S(1)}, f32[96,128]{1,0:T(8,128)S(1)}, u32[]{:S(2)}, u32[]{:S(2)}) collective-permute-start(f32[96,128]{1,0:T(8,128)S(1)} %get-tuple-element.20), channel_id=1, source_target_pairs={{0,1},{1,0},{2,3},{3,2},{4,5},{5,4},{6,7},{7,6},{8,9},{9,8},{10,11... | collective-permute-start | bytes 147464 | tf_op jit(solution)/shard_map/ppermute | solution.py:150
  21.0 9.7 %collective-permute-start.4 = (f32[192,128]{1,0:T(8,128)S(1)}, f32[192,128]{1,0:T(8,128)S(1)}, u32[]{:S(2)}, u32[]{:S(2)}) collective-permute-start(f32[192,128]{1,0:T(8,128)S(1)} %shard_map.39.refs_0_), channel_id=1, source_target_pairs={{0,4},{1,5},{2,6},{3,7},{4,0},{5,1},{6,2},{7,3},{8,12},{9,13},{10,... | collective-permute-start | bytes 294920 | tf_op jit(solution)/shard_map/ppermute | solution.py:150
  23.6 4.2 %collective-permute-start.12 = (f32[96,128]{1,0:T(8,128)S(1)}, f32[96,128]{1,0:T(8,128)S(1)}, u32[]{:S(2)}, u32[]{:S(2)}) collective-permute-start(f32[96,128]{1,0:T(8,128)S(1)} %get-tuple-element.23.refs_0_), channel_id=1, source_target_pairs={{0,2},{1,3},{2,0},{3,1},{4,6},{5,7},{6,4},{7,5},{8,10},{9,11},{10,... | collective-permute-start | bytes 147464 | tf_op jit(solution)/shard_map/ppermute | solution.py:150
  25.3 6.4 %collective-permute-start.14 = (f32[96,128]{1,0:T(8,128)S(1)}, f32[96,128]{1,0:T(8,128)S(1)}, u32[]{:S(2)}, u32[]{:S(2)}) collective-permute-start(f32[96,128]{1,0:T(8,128)S(1)} %get-tuple-element.24.refs_0_), channel_id=1, source_target_pairs={{0,4},{1,5},{2,6},{3,7},{4,0},{5,1},{6,2},{7,3},{8,12},{9,13},{10,... | collective-permute-start | bytes 147464 | tf_op jit(solution)/shard_map/ppermute | solution.py:150
  27.8 5.6 %collective-permute-start.16 = (f32[96,128]{1,0:T(8,128)S(1)}, f32[96,128]{1,0:T(8,128)S(1)}, u32[]{:S(2)}, u32[]{:S(2)}) collective-permute-start(f32[96,128]{1,0:T(8,128)S(1)} %shard_map.45.refs_2_.refs_0_), channel_id=1, source_target_pairs={{0,4},{1,5},{2,6},{3,7},{4,0},{5,1},{6,2},{7,3},{8,12},{9,13},{10,... | collective-permute-start | bytes 147464 | tf_op jit(solution)/shard_map/ppermute | solution.py:150
  30.7 2.8 %collective-permute-start.13 = (bf16[192,128]{1,0:T(8,128)(2,1)S(1)}, bf16[192,128]{1,0:T(8,128)(2,1)S(1)}, u32[]{:S(2)}, u32[]{:S(2)}) collective-permute-start(bf16[192,128]{1,0:T(8,128)(2,1)S(1)} %shard_map.47.refs_4_), channel_id=1, source_target_pairs={{0,1},{1,0},{2,3},{3,2},{4,5},{5,4},{6,7},{7,6},{8,9},{9,8},{10,11... | collective-permute-start | bytes 147464 | tf_op jit(solution)/shard_map/ppermute | solution.py:150
  31.8 1.7 %collective-permute-start.15 = (bf16[96,128]{1,0:T(8,128)(2,1)S(1)}, bf16[96,128]{1,0:T(8,128)(2,1)S(1)}, u32[]{:S(2)}, u32[]{:S(2)}) collective-permute-start(bf16[96,128]{1,0:T(8,128)(2,1)S(1)} %shard_map.48.refs_8_), channel_id=1, source_target_pairs={{0,1},{1,0},{2,3},{3,2},{4,5},{5,4},{6,7},{7,6},{8,9},{9,8},{10,11... | collective-permute-start | bytes 73736 | tf_op jit(solution)/shard_map/ppermute | solution.py:150
  33.4 1.3 %collective-permute-start.17 = (bf16[96,128]{1,0:T(8,128)(2,1)S(1)}, bf16[96,128]{1,0:T(8,128)(2,1)S(1)}, u32[]{:S(2)}, u32[]{:S(2)}) collective-permute-start(bf16[96,128]{1,0:T(8,128)(2,1)S(1)} %shard_map.50.mine_ref), channel_id=1, source_target_pairs={{0,1},{1,0},{2,3},{3,2},{4,5},{5,4},{6,7},{7,6},{8,9},{9,8},{10,11... | collective-permute-start | bytes 73736 | tf_op jit(solution)/shard_map/ppermute | solution.py:150

commit v6 on v3

--- a/solution.py
+++ b/solution.py
@@ -134,7 +134,7 @@
 
 def finish(acc, group, mine, theirs, turned):
     rows, cols = acc.shape[0], mine.shape[1]
-    chunk = rows // 3 if rows % 48 == 0 else rows
+    chunk = rows // 2 if rows % 32 == 0 else rows
     shapes = [(piece.shape[0], piece.shape[2]) for piece, _, _ in group]
     return pl.pallas_call(
         functools.partial(finish_body, shapes, chunk),

time: 35.9 us -> 36 us (level)
  no operation moved by 1% of the time
where the time goes in v6:
time: 36 us; the launch traced here: 35.8 us
  starting transfers between devices  21 us (58%)
  waiting for transfers between devices  10.2 us (28%)
  Pallas kernels  3.34 us (9%)
  local copies, waits for them, and re-layouts  1.15 us (3%)
    ppermute x18, starting transfers between devices, swap(): return lax.ppermute(x, axis, [(i, i ^ bit) for i in range(size)])  21 us
    ppermute x18, waiting for transfers between devices, swap(): return lax.ppermute(x, axis, [(i, i ^ bit) for i in range(size)])  10.2 us
    pallas_call x14, Pallas kernels, call(): pl.pallas_call(kernel, out_shape=outs, in_specs=[VMEM] * given + [ANY] *...  2.19 us
    pallas_call x1, Pallas kernels, finish(): pl.pallas_call(functools.partial(finish_body, shapes, chunk), out_shape=j...  1.15 us
    slice x1, local copies, waits for them, and re-layouts, on_square(): low, high = (own[:, :, :half], own[:, :, half:])  1.14 us
  transfers between devices with their start and end apart: 18, of which 9 were waited for; matrix products, arithmetic and copies ran while one was open for 0% of the time, Pallas kernels for 6%

profile of v6, /device:TPU:0, one launch (start us, length us, event | category | flops | bytes accessed | tf_op | source)
XLA Modules:
  0.0 35.8 jit_solution(10383290957124864222)
XLA Ops:
  0.0 1.1 %fusion = (bf16[3,2,16,1152]{3,2,1,0:T(8,128)(2,1)S(1)}, bf16[3,2,16,1152]{3,2,1,0:T(8,128)(2,1)S(1)}) fusion(bf16[3,2,32,1152]{3,2,1,0:T(8,128)(2,1)} %bitcast.1), kind=kLoop, calls=%fused_computation | loop fusion | bytes 884736 | tf_op jit(solution)/shard_map/slice | solution.py:216
  1.1 3.0 %collective-permute-start.1 = (bf16[3,2,16,1152]{3,2,1,0:T(8,128)(2,1)S(1)}, bf16[3,2,16,1152]{3,2,1,0:T(8,128)(2,1)S(1)}, u32[]{:S(2)}, u32[]{:S(2)}) collective-permute-start(bf16[3,2,16,1152]{3,2,1,0:T(8,128)(2,1)S(1)} %get-tuple-element.27.refs_1_), channel_id=1, source_target_pairs={{0,16},{8,24},{16,0},{24,8},{1,17},{9,25},{17,1},{25,9},{2,18},{10... | collective-permute-start | bytes 663560 | tf_op jit(solution)/shard_map/ppermute | solution.py:150
  4.2 1.5 %collective-permute-start = (bf16[3,2,16,1152]{3,2,1,0:T(8,128)(2,1)S(1)}, bf16[3,2,16,1152]{3,2,1,0:T(8,128)(2,1)S(1)}, u32[]{:S(2)}, u32[]{:S(2)}) collective-permute-start(bf16[3,2,16,1152]{3,2,1,0:T(8,128)(2,1)S(1)} %get-tuple-element.28.refs_0_), channel_id=1, source_target_pairs={{0,8},{8,0},{16,24},{24,16},{1,9},{9,1},{17,25},{25,17},{2,10},{10... | collective-permute-start | bytes 663560 | tf_op jit(solution)/shard_map/ppermute | solution.py:150
  5.7 0.5 %collective-permute-start.8 = (bf16[3,2,16,1152]{3,2,1,0:T(8,128)(2,1)S(1)}, bf16[3,2,16,1152]{3,2,1,0:T(8,128)(2,1)S(1)}, u32[]{:S(2)}, u32[]{:S(2)}) collective-permute-start(bf16[3,2,16,1152]{3,2,1,0:T(8,128)(2,1)S(1)} %get-tuple-element.27.refs_1_), channel_id=1, source_target_pairs={{0,8},{8,0},{16,24},{24,16},{1,9},{9,1},{17,25},{25,17},{2,10},{10... | collective-permute-start | bytes 663560 | tf_op jit(solution)/shard_map/ppermute | solution.py:150
  6.2 0.1 collective-permute-start.9
  6.3 4.2 %collective-permute-done.1.refs_3_ = bf16[3,2,16,1152]{3,2,1,0:T(8,128)(2,1)S(1)} collective-permute-done((bf16[3,2,16,1152]{3,2,1,0:T(8,128)(2,1)S(1)}, bf16[3,2,16,1152]{3,2,1,0:T(8,128)(2,1)S(1)}, u32[]{:S(2)}, u32[]{:S(2)}) %collective-permute-start.1) | collective-permute-done | bytes 221216 | tf_op jit(solution)/shard_map/ppermute | solution.py:150
  10.4 2.0 %collective-permute-start.6 = (bf16[3,2,16,1152]{3,2,1,0:T(8,128)(2,1)S(1)}, bf16[3,2,16,1152]{3,2,1,0:T(8,128)(2,1)S(1)}, u32[]{:S(2)}, u32[]{:S(2)}) collective-permute-start(bf16[3,2,16,1152]{3,2,1,0:T(8,128)(2,1)S(1)} %collective-permute-done.1.refs_3_), channel_id=1, source_target_pairs={{0,8},{8,0},{16,24},{24,16},{1,9},{9,1},{17,25},{25,17},{2,10},{10... | collective-permute-start | bytes 663560 | tf_op jit(solution)/shard_map/ppermute | solution.py:150
  12.5 1.5 %collective-permute-start.5 = (bf16[3,2,16,1152]{3,2,1,0:T(8,128)(2,1)S(1)}, bf16[3,2,16,1152]{3,2,1,0:T(8,128)(2,1)S(1)}, u32[]{:S(2)}, u32[]{:S(2)}) collective-permute-start(bf16[3,2,16,1152]{3,2,1,0:T(8,128)(2,1)S(1)} %collective-permute-done.refs_2_), channel_id=1, source_target_pairs={{0,16},{8,24},{16,0},{24,8},{1,17},{9,25},{17,1},{25,9},{2,18},{10... | collective-permute-start | bytes 663560 | tf_op jit(solution)/shard_map/ppermute | solution.py:150
  14.0 0.4 %shard_map.37 = (f32[192,128]{1,0:T(8,128)S(1)}, f32[192,128]{1,0:T(8,128)S(1)}) custom-call(bf16[3,2,16,1152]{3,2,1,0:T(8,128)(2,1)S(1)} %get-tuple-element.28.refs_0_, bf16[3,2,16,1152]{3,2,1,0:T(8,128)(2,1)S(1)} %get-tuple-element.27.refs_1_, bf16[3,2,16,1152]{3,2,1,0:T(8,128)(2,1)S(1)} %collective-permute-done.refs_2_, ...), custom_call_target="tpu_custom_call" | custom-call | flops 226492416 | bytes 1671168 | tf_op jit(solution)/shard_map/pallas_call | solution.py:23
  14.4 0.1 collective-permute-start.2
  14.5 1.3 %collective-permute-done.2.refs_1_ = f32[192,128]{1,0:T(8,128)S(1)} collective-permute-done((f32[192,128]{1,0:T(8,128)S(1)}, f32[192,128]{1,0:T(8,128)S(1)}, u32[]{:S(2)}, u32[]{:S(2)}) %collective-permute-start.2) | collective-permute-done | bytes 98336 | tf_op jit(solution)/shard_map/ppermute | solution.py:150
  15.8 1.6 %collective-permute-start.3 = (f32[192,128]{1,0:T(8,128)S(1)}, f32[192,128]{1,0:T(8,128)S(1)}, u32[]{:S(2)}, u32[]{:S(2)}) collective-permute-start(f32[192,128]{1,0:T(8,128)S(1)} %shard_map.38.refs_0_), channel_id=1, source_target_pairs={{0,2},{1,3},{2,0},{3,1},{4,6},{5,7},{6,4},{7,5},{8,10},{9,11},{10,... | collective-permute-start | bytes 294920 | tf_op jit(solution)/shard_map/ppermute | solution.py:150
  17.5 0.3 shard_map.42
  17.8 0.1 collective-permute-start.10
  17.9 1.2 %collective-permute-done.10.refs_1_ = f32[96,128]{1,0:T(8,128)S(1)} collective-permute-done((f32[96,128]{1,0:T(8,128)S(1)}, f32[96,128]{1,0:T(8,128)S(1)}, u32[]{:S(2)}, u32[]{:S(2)}) %collective-permute-start.10) | collective-permute-done | bytes 49184 | tf_op jit(solution)/shard_map/ppermute | solution.py:150
  19.1 1.4 %collective-permute-start.11 = (f32[96,128]{1,0:T(8,128)S(1)}, f32[96,128]{1,0:T(8,128)S(1)}, u32[]{:S(2)}, u32[]{:S(2)}) collective-permute-start(f32[96,128]{1,0:T(8,128)S(1)} %shard_map.43.refs_2_), channel_id=1, source_target_pairs={{0,2},{1,3},{2,0},{3,1},{4,6},{5,7},{6,4},{7,5},{8,10},{9,11},{10,... | collective-permute-start | bytes 147464 | tf_op jit(solution)/shard_map/ppermute | solution.py:150
  20.6 0.3 shard_map.41
  20.9 0.1 collective-permute-start.7
  21.0 2.7 %collective-permute-start.4 = (f32[192,128]{1,0:T(8,128)S(1)}, f32[192,128]{1,0:T(8,128)S(1)}, u32[]{:S(2)}, u32[]{:S(2)}) collective-permute-start(f32[192,128]{1,0:T(8,128)S(1)} %shard_map.39.refs_0_), channel_id=1, source_target_pairs={{0,4},{1,5},{2,6},{3,7},{4,0},{5,1},{6,2},{7,3},{8,12},{9,13},{10,... | collective-permute-start | bytes 294920 | tf_op jit(solution)/shard_map/ppermute | solution.py:150
  23.6 1.6 %collective-permute-start.15 = (f32[96,128]{1,0:T(8,128)S(1)}, f32[96,128]{1,0:T(8,128)S(1)}, u32[]{:S(2)}, u32[]{:S(2)}) collective-permute-start(f32[96,128]{1,0:T(8,128)S(1)} %get-tuple-element.23.refs_2_.refs_0_), channel_id=1, source_target_pairs={{0,2},{1,3},{2,0},{3,1},{4,6},{5,7},{6,4},{7,5},{8,10},{9,11},{10,... | collective-permute-start | bytes 147464 | tf_op jit(solution)/shard_map/ppermute | solution.py:150
  25.3 2.0 %collective-permute-start.13 = (f32[96,128]{1,0:T(8,128)S(1)}, f32[96,128]{1,0:T(8,128)S(1)}, u32[]{:S(2)}, u32[]{:S(2)}) collective-permute-start(f32[96,128]{1,0:T(8,128)S(1)} %get-tuple-element.24.refs_0_), channel_id=1, source_target_pairs={{0,4},{1,5},{2,6},{3,7},{4,0},{5,1},{6,2},{7,3},{8,12},{9,13},{10,... | collective-permute-start | bytes 147464 | tf_op jit(solution)/shard_map/ppermute | solution.py:150
  27.3 0.1 shard_map.40
  27.5 0.2 shard_map.45.refs_3_.turned
  27.7 0.1 collective-permute-done.15.refs_1_
  27.8 2.6 %collective-permute-start.16 = (f32[96,128]{1,0:T(8,128)S(1)}, f32[96,128]{1,0:T(8,128)S(1)}, u32[]{:S(2)}, u32[]{:S(2)}) collective-permute-start(f32[96,128]{1,0:T(8,128)S(1)} %shard_map.49.refs_0_), channel_id=1, source_target_pairs={{0,4},{1,5},{2,6},{3,7},{4,0},{5,1},{6,2},{7,3},{8,12},{9,13},{10,... | collective-permute-start | bytes 147464 | tf_op jit(solution)/shard_map/ppermute | solution.py:150
  30.4 0.3 collective-permute-done.4.refs_1_
  30.8 0.9 %collective-permute-done.13.refs_1_ = f32[96,128]{1,0:T(8,128)S(1)} collective-permute-done((f32[96,128]{1,0:T(8,128)S(1)}, f32[96,128]{1,0:T(8,128)S(1)}, u32[]{:S(2)}, u32[]{:S(2)}) %collective-permute-start.13) | collective-permute-done | bytes 49184 | tf_op jit(solution)/shard_map/ppermute | solution.py:150
  31.8 0.1 collective-permute-start.14
  31.8 1.6 %collective-permute-done.16.refs_1_ = f32[96,128]{1,0:T(8,128)S(1)} collective-permute-done((f32[96,128]{1,0:T(8,128)S(1)}, f32[96,128]{1,0:T(8,128)S(1)}, u32[]{:S(2)}, u32[]{:S(2)}) %collective-permute-start.16) | collective-permute-done | bytes 49184 | tf_op jit(solution)/shard_map/ppermute | solution.py:150
  33.5 0.7 %shard_map.48.acc = f32[1152,256]{1,0:T(8,128)S(1)} custom-call(bf16[3,2,16,1152]{3,2,1,0:T(8,128)(2,1)S(1)} %get-tuple-element.28.refs_0_, bf16[3,2,16,1152]{3,2,1,0:T(8,128)(2,1)S(1)} %get-tuple-element.27.refs_1_, bf16[3,2,16,1152]{3,2,1,0:T(8,128)(2,1)S(1)} %collective-permute-done.refs_2_, bf16[3,2,16,1152]{3,2,1,0:T(8,128)(2,1)S(1)} %collective-permute-done.1.refs_3_, ...), custom_call_target="tpu_custom_call" | custom-call | flops 339738624 | bytes 2654208 | tf_op jit(solution)/shard_map/pallas_call | solution.py:23
  34.2 0.5 %collective-permute-done.17.theirs_ref = bf16[96,128]{1,0:T(8,128)(2,1)S(1)} collective-permute-done((bf16[96,128]{1,0:T(8,128)(2,1)S(1)}, bf16[96,128]{1,0:T(8,128)(2,1)S(1)}, u32[]{:S(2)}, u32[]{:S(2)}) %collective-permute-start.17) | collective-permute-done | bytes 24608 | tf_op jit(solution)/shard_map/ppermute | solution.py:150
  34.7 1.2 %shard_map.51 = bf16[2,1152,128]{2,1,0:T(8,128)(2,1)} custom-call(f32[1152,256]{1,0:T(8,128)S(1)} %shard_map.48.acc, bf16[1152,192]{1,0:T(8,128)(2,1)S(1)} %shard_map.45.refs_3_.turned, bf16[96,128]{1,0:T(8,128)(2,1)S(1)} %shard_map.50.mine_ref, bf16[96,128]{1,0:T(8,128)(2,1)S(1)} %collective-permute-done.17.theirs_ref), custom_call_target="tpu_custom_call" | custom-call | tf_op jit(solution)/shard_map/pallas_call | solution.py:139
  (24 shorter events, 0.4 us)
Async XLA Ops:
  0.0 14.0 %copy-start = (bf16[2,1152,128]{2,1,0:T(8,128)(2,1)S(1)}, bf16[2,1152,128]{2,1,0:T(8,128)(2,1)}, u32[]{:S(2)}) copy-start(bf16[2,1152,128]{2,1,0:T(8,128)(2,1)} %refs_2_.3) | copy-start | bytes 1769476
  1.1 9.3 %collective-permute-start.1 = (bf16[3,2,16,1152]{3,2,1,0:T(8,128)(2,1)S(1)}, bf16[3,2,16,1152]{3,2,1,0:T(8,128)(2,1)S(1)}, u32[]{:S(2)}, u32[]{:S(2)}) collective-permute-start(bf16[3,2,16,1152]{3,2,1,0:T(8,128)(2,1)S(1)} %get-tuple-element.27.refs_1_), channel_id=1, source_target_pairs={{0,16},{8,24},{16,0},{24,8},{1,17},{9,25},{17,1},{25,9},{2,18},{10... | collective-permute-start | bytes 663560 | tf_op jit(solution)/shard_map/ppermute | solution.py:150
  4.2 8.4 %collective-permute-start = (bf16[3,2,16,1152]{3,2,1,0:T(8,128)(2,1)S(1)}, bf16[3,2,16,1152]{3,2,1,0:T(8,128)(2,1)S(1)}, u32[]{:S(2)}, u32[]{:S(2)}) collective-permute-start(bf16[3,2,16,1152]{3,2,1,0:T(8,128)(2,1)S(1)} %get-tuple-element.28.refs_0_), channel_id=1, source_target_pairs={{0,8},{8,0},{16,24},{24,16},{1,9},{9,1},{17,25},{25,17},{2,10},{10... | collective-permute-start | bytes 663560 | tf_op jit(solution)/shard_map/ppermute | solution.py:150
  5.7 11.8 %collective-permute-start.8 = (bf16[3,2,16,1152]{3,2,1,0:T(8,128)(2,1)S(1)}, bf16[3,2,16,1152]{3,2,1,0:T(8,128)(2,1)S(1)}, u32[]{:S(2)}, u32[]{:S(2)}) collective-permute-start(bf16[3,2,16,1152]{3,2,1,0:T(8,128)(2,1)S(1)} %get-tuple-element.27.refs_1_), channel_id=1, source_target_pairs={{0,8},{8,0},{16,24},{24,16},{1,9},{9,1},{17,25},{25,17},{2,10},{10... | collective-permute-start | bytes 663560 | tf_op jit(solution)/shard_map/ppermute | solution.py:150
  6.2 11.3 %collective-permute-start.9 = (bf16[3,2,16,1152]{3,2,1,0:T(8,128)(2,1)S(1)}, bf16[3,2,16,1152]{3,2,1,0:T(8,128)(2,1)S(1)}, u32[]{:S(2)}, u32[]{:S(2)}) collective-permute-start(bf16[3,2,16,1152]{3,2,1,0:T(8,128)(2,1)S(1)} %get-tuple-element.28.refs_0_), channel_id=1, source_target_pairs={{0,16},{8,24},{16,0},{24,8},{1,17},{9,25},{17,1},{25,9},{2,18},{10... | collective-permute-start | bytes 663560 | tf_op jit(solution)/shard_map/ppermute | solution.py:150
  10.4 10.1 %collective-permute-start.6 = (bf16[3,2,16,1152]{3,2,1,0:T(8,128)(2,1)S(1)}, bf16[3,2,16,1152]{3,2,1,0:T(8,128)(2,1)S(1)}, u32[]{:S(2)}, u32[]{:S(2)}) collective-permute-start(bf16[3,2,16,1152]{3,2,1,0:T(8,128)(2,1)S(1)} %collective-permute-done.1.refs_3_), channel_id=1, source_target_pairs={{0,8},{8,0},{16,24},{24,16},{1,9},{9,1},{17,25},{25,17},{2,10},{10... | collective-permute-start | bytes 663560 | tf_op jit(solution)/shard_map/ppermute | solution.py:150
  12.5 8.0 %collective-permute-start.5 = (bf16[3,2,16,1152]{3,2,1,0:T(8,128)(2,1)S(1)}, bf16[3,2,16,1152]{3,2,1,0:T(8,128)(2,1)S(1)}, u32[]{:S(2)}, u32[]{:S(2)}) collective-permute-start(bf16[3,2,16,1152]{3,2,1,0:T(8,128)(2,1)S(1)} %collective-permute-done.refs_2_), channel_id=1, source_target_pairs={{0,16},{8,24},{16,0},{24,8},{1,17},{9,25},{17,1},{25,9},{2,18},{10... | collective-permute-start | bytes 663560 | tf_op jit(solution)/shard_map/ppermute | solution.py:150
  14.4 1.4 %collective-permute-start.2 = (f32[192,128]{1,0:T(8,128)S(1)}, f32[192,128]{1,0:T(8,128)S(1)}, u32[]{:S(2)}, u32[]{:S(2)}) collective-permute-start(f32[192,128]{1,0:T(8,128)S(1)} %get-tuple-element.17), channel_id=1, source_target_pairs={{0,1},{1,0},{2,3},{3,2},{4,5},{5,4},{6,7},{7,6},{8,9},{9,8},{10,11... | collective-permute-start | bytes 294920 | tf_op jit(solution)/shard_map/ppermute | solution.py:150
  15.8 11.5 %copy-start.1 = (f32[3,128]{1,0:T(4,128)S(1)}, f32[3,128]{1,0:T(4,128)}, u32[]{:S(2)}) copy-start(f32[3,128]{1,0:T(4,128)} %refs_0_.1) | copy-start | bytes 4612
  15.8 5.1 %collective-permute-start.3 = (f32[192,128]{1,0:T(8,128)S(1)}, f32[192,128]{1,0:T(8,128)S(1)}, u32[]{:S(2)}, u32[]{:S(2)}) collective-permute-start(f32[192,128]{1,0:T(8,128)S(1)} %shard_map.38.refs_0_), channel_id=1, source_target_pairs={{0,2},{1,3},{2,0},{3,1},{4,6},{5,7},{6,4},{7,5},{8,10},{9,11},{10,... | collective-permute-start | bytes 294920 | tf_op jit(solution)/shard_map/ppermute | solution.py:150
  17.8 1.3 %collective-permute-start.10 = (f32[96,128]{1,0:T(8,128)S(1)}, f32[96,128]{1,0:T(8,128)S(1)}, u32[]{:S(2)}, u32[]{:S(2)}) collective-permute-start(f32[96,128]{1,0:T(8,128)S(1)} %get-tuple-element.22), channel_id=1, source_target_pairs={{0,1},{1,0},{2,3},{3,2},{4,5},{5,4},{6,7},{7,6},{8,9},{9,8},{10,11... | collective-permute-start | bytes 147464 | tf_op jit(solution)/shard_map/ppermute | solution.py:150
  19.1 4.5 %collective-permute-start.11 = (f32[96,128]{1,0:T(8,128)S(1)}, f32[96,128]{1,0:T(8,128)S(1)}, u32[]{:S(2)}, u32[]{:S(2)}) collective-permute-start(f32[96,128]{1,0:T(8,128)S(1)} %shard_map.43.refs_2_), channel_id=1, source_target_pairs={{0,2},{1,3},{2,0},{3,1},{4,6},{5,7},{6,4},{7,5},{8,10},{9,11},{10,... | collective-permute-start | bytes 147464 | tf_op jit(solution)/shard_map/ppermute | solution.py:150
  20.9 2.8 %collective-permute-start.7 = (f32[96,128]{1,0:T(8,128)S(1)}, f32[96,128]{1,0:T(8,128)S(1)}, u32[]{:S(2)}, u32[]{:S(2)}) collective-permute-start(f32[96,128]{1,0:T(8,128)S(1)} %get-tuple-element.20), channel_id=1, source_target_pairs={{0,1},{1,0},{2,3},{3,2},{4,5},{5,4},{6,7},{7,6},{8,9},{9,8},{10,11... | collective-permute-start | bytes 147464 | tf_op jit(solution)/shard_map/ppermute | solution.py:150
  21.0 9.7 %collective-permute-start.4 = (f32[192,128]{1,0:T(8,128)S(1)}, f32[192,128]{1,0:T(8,128)S(1)}, u32[]{:S(2)}, u32[]{:S(2)}) collective-permute-start(f32[192,128]{1,0:T(8,128)S(1)} %shard_map.39.refs_0_), channel_id=1, source_target_pairs={{0,4},{1,5},{2,6},{3,7},{4,0},{5,1},{6,2},{7,3},{8,12},{9,13},{10,... | collective-permute-start | bytes 294920 | tf_op jit(solution)/shard_map/ppermute | solution.py:150
  23.6 4.2 %collective-permute-start.15 = (f32[96,128]{1,0:T(8,128)S(1)}, f32[96,128]{1,0:T(8,128)S(1)}, u32[]{:S(2)}, u32[]{:S(2)}) collective-permute-start(f32[96,128]{1,0:T(8,128)S(1)} %get-tuple-element.23.refs_2_.refs_0_), channel_id=1, source_target_pairs={{0,2},{1,3},{2,0},{3,1},{4,6},{5,7},{6,4},{7,5},{8,10},{9,11},{10,... | collective-permute-start | bytes 147464 | tf_op jit(solution)/shard_map/ppermute | solution.py:150
  25.3 6.4 %collective-permute-start.13 = (f32[96,128]{1,0:T(8,128)S(1)}, f32[96,128]{1,0:T(8,128)S(1)}, u32[]{:S(2)}, u32[]{:S(2)}) collective-permute-start(f32[96,128]{1,0:T(8,128)S(1)} %get-tuple-element.24.refs_0_), channel_id=1, source_target_pairs={{0,4},{1,5},{2,6},{3,7},{4,0},{5,1},{6,2},{7,3},{8,12},{9,13},{10,... | collective-permute-start | bytes 147464 | tf_op jit(solution)/shard_map/ppermute | solution.py:150
  27.8 5.6 %collective-permute-start.16 = (f32[96,128]{1,0:T(8,128)S(1)}, f32[96,128]{1,0:T(8,128)S(1)}, u32[]{:S(2)}, u32[]{:S(2)}) collective-permute-start(f32[96,128]{1,0:T(8,128)S(1)} %shard_map.49.refs_0_), channel_id=1, source_target_pairs={{0,4},{1,5},{2,6},{3,7},{4,0},{5,1},{6,2},{7,3},{8,12},{9,13},{10,... | collective-permute-start | bytes 147464 | tf_op jit(solution)/shard_map/ppermute | solution.py:150
  30.7 2.8 %collective-permute-start.12 = (bf16[192,128]{1,0:T(8,128)(2,1)S(1)}, bf16[192,128]{1,0:T(8,128)(2,1)S(1)}, u32[]{:S(2)}, u32[]{:S(2)}) collective-permute-start(bf16[192,128]{1,0:T(8,128)(2,1)S(1)} %shard_map.46.refs_4_), channel_id=1, source_target_pairs={{0,1},{1,0},{2,3},{3,2},{4,5},{5,4},{6,7},{7,6},{8,9},{9,8},{10,11... | collective-permute-start | bytes 147464 | tf_op jit(solution)/shard_map/ppermute | solution.py:150
  31.8 1.7 %collective-permute-start.14 = (bf16[96,128]{1,0:T(8,128)(2,1)S(1)}, bf16[96,128]{1,0:T(8,128)(2,1)S(1)}, u32[]{:S(2)}, u32[]{:S(2)}) collective-permute-start(bf16[96,128]{1,0:T(8,128)(2,1)S(1)} %shard_map.47.refs_8_), channel_id=1, source_target_pairs={{0,1},{1,0},{2,3},{3,2},{4,5},{5,4},{6,7},{7,6},{8,9},{9,8},{10,11... | collective-permute-start | bytes 73736 | tf_op jit(solution)/shard_map/ppermute | solution.py:150
  33.4 1.3 %collective-permute-start.17 = (bf16[96,128]{1,0:T(8,128)(2,1)S(1)}, bf16[96,128]{1,0:T(8,128)(2,1)S(1)}, u32[]{:S(2)}, u32[]{:S(2)}) collective-permute-start(bf16[96,128]{1,0:T(8,128)(2,1)S(1)} %shard_map.50.mine_ref), channel_id=1, source_target_pairs={{0,1},{1,0},{2,3},{3,2},{4,5},{5,4},{6,7},{7,6},{8,9},{9,8},{10,11... | collective-permute-start | bytes 73736 | tf_op jit(solution)/shard_map/ppermute | solution.py:150
